TPU v7x, 32 devices: a whole 2x2x4 slice. The times are simulated.
32 devices in a mesh: row: 4 (over y, x), col: 8 (over z, core).
Axes of the slice: x: 2, y: 2, z: 4, core: 2. Of those that a mesh axis runs over, the one named last changes fastest.
Arguments:
- features: bfloat16 [8192, 256], P(('col', 'row')), may hold values from -6 to 6
- cotangent: bfloat16 [8192, 256], P(('row', 'col')), may hold values from -1.5 to 1.5
- degrees: int32 [8192], P(('row', 'col')), may hold values from 8 to 40
- weight: bfloat16 [256, 256], replicated, may hold values from -0.375 to 0.375
- tile_rows: int32 [4, 8, 256], P('row', 'col'), may hold values from 0 to 15
- tile_cols: int32 [4, 8, 256], P('row', 'col'), may hold values from 0 to 7
- tile_bits: int32 [4, 8, 256, 16, 128], P('row', 'col'), may hold values from 0 to 255, as said below
- tile_count: int32 [4, 8], P('row', 'col'), may hold values from 16 to 256, as said below
Outputs:
- output: bfloat16 [8192, 256], P(('row', 'col'))
- weight_grad: float32 [256, 256], replicated
- input_grad: bfloat16 [8192, 256], P(('col', 'row'))
Inputs may be any that keep to these rules, and one draw needn't show every extreme that they name: `tile_bits`: each word holds 8 entries of 0 or 1 in its low bits; tiles at the same position may repeat and then add. `tile_count`: some device has all 256 slots live and some device 256 // 16.
All inputs are finite; a program needn't handle non-finite values.
Results may differ from a plain program's by a relative error of at most 0.024.
Values may be sent and summed in bfloat16 or wider, within the bound.
A program may use at most 64 MiB of HBM per device.

v0:
```python
import math

import jax
import jax.numpy as jnp
from jax import lax
from jax.sharding import PartitionSpec as P


def unpack(packed):
    shifts = jnp.arange(8, dtype=jnp.int32)
    flags = jnp.right_shift(packed[:, :, None, :], shifts[None, None, :, None]) & 1
    return flags.reshape(packed.shape[0], packed.shape[1] * 8, packed.shape[2])


def sweep_tiles(packed, row_ids, col_ids, live_count, source, tile_offset, out_tiles, forward):
    tile_size = packed.shape[-1]
    feature_width = source.shape[-1]
    block_size = math.gcd(packed.shape[0], 32)

    def one_block(position, totals):
        offset = position * block_size
        block_bits = lax.dynamic_slice_in_dim(packed, offset, block_size, 0)
        block_rows = lax.dynamic_slice_in_dim(row_ids, offset, block_size, 0)
        block_cols = lax.dynamic_slice_in_dim(col_ids, offset, block_size, 0)
        if forward:
            target = block_rows - tile_offset
        else:
            target = block_cols - tile_offset
        inside = (target >= 0) & (target < out_tiles)
        live_mask = (offset + jnp.arange(block_size, dtype=jnp.int32) < live_count) & inside
        placed = jnp.clip(target, 0, out_tiles - 1)
        pattern = (unpack(block_bits) * live_mask.astype(jnp.int32)[:, None, None]).astype(
            jnp.bfloat16
        )
        if forward:
            product = jnp.einsum(
                "bji,bjf->bif", pattern, source[block_cols], preferred_element_type=jnp.float32
            )
        else:
            product = jnp.einsum(
                "bji,bif->bjf", pattern, source[block_rows], preferred_element_type=jnp.float32
            )
        return totals.at[placed].add(product)

    initial = jnp.zeros((out_tiles, tile_size, feature_width), jnp.float32)
    blocks_used = packed.shape[0] // block_size
    return lax.fori_loop(0, blocks_used, one_block, initial)


def forward_pass(features, degrees, weight, packed, row_ids, col_ids, live_count):
    tile_size = packed.shape[-1]
    width = features.shape[-1]
    gathered = lax.all_gather(features, "row", axis=0, tiled=True)
    source = gathered.reshape(-1, tile_size, width)
    out_tiles = features.shape[0] * lax.axis_size("col") // tile_size
    partial_value = sweep_tiles(packed, row_ids, col_ids, live_count, source, 0, out_tiles, True)
    summed = lax.psum_scatter(
        partial_value.reshape(-1, width).astype(jnp.bfloat16),
        "col",
        scatter_dimension=0,
        tiled=True,
    ).astype(jnp.float32)
    aggregated = (summed / degrees[:, None].astype(jnp.float32)).astype(jnp.bfloat16)
    output = jnp.dot(aggregated, weight, preferred_element_type=jnp.float32).astype(jnp.bfloat16)
    return (aggregated, output)


def backward_pass(cotangent, degrees, weight, packed, row_ids, col_ids, live_count):
    tile_size = packed.shape[-1]
    width = cotangent.shape[-1]
    scaled = (cotangent.astype(jnp.float32) / degrees[:, None].astype(jnp.float32)).astype(
        jnp.bfloat16
    )
    gathered = lax.all_gather(scaled, "col", axis=0, tiled=True)
    source = gathered.reshape(-1, tile_size, width)
    out_tiles = cotangent.shape[0] * lax.axis_size("row") // tile_size
    partial_value = sweep_tiles(packed, row_ids, col_ids, live_count, source, 0, out_tiles, False)
    summed = lax.psum_scatter(
        partial_value.reshape(-1, width).astype(jnp.bfloat16),
        "row",
        scatter_dimension=0,
        tiled=True,
    )
    return jnp.dot(summed, weight.T, preferred_element_type=jnp.float32).astype(jnp.bfloat16)


def per_device(features, cotangent, degrees, weight, tile_rows, tile_cols, tile_bits, tile_count):
    packed = tile_bits[0, 0]
    row_ids = tile_rows[0, 0]
    col_ids = tile_cols[0, 0]
    live_count = tile_count[0, 0]
    aggregated, output = forward_pass(
        features, degrees, weight, packed, row_ids, col_ids, live_count
    )
    input_grad = backward_pass(cotangent, degrees, weight, packed, row_ids, col_ids, live_count)
    local_term = lax.dot_general(
        aggregated, cotangent, (((0,), (0,)), ((), ())), preferred_element_type=jnp.float32
    )
    weight_grad = lax.psum(local_term, ("row", "col"))
    return (output, weight_grad, input_grad)


def solution(mesh):
    placed = (
        P(("col", "row"), None),
        P(("row", "col"), None),
        P(("row", "col")),
        P(),
        P("row", "col", None),
        P("row", "col", None),
        P("row", "col", None, None, None),
        P("row", "col"),
    )
    return jax.shard_map(
        per_device,
        mesh=mesh,
        in_specs=placed,
        out_specs=(P(("row", "col"), None), P(), P(("col", "row"), None)),
        check_vma=False,
    )
```

profile of v0, /device:TPU:0, one launch (start us, length us, event | category | flops | bytes accessed | tf_op | source)
XLA Modules:
  0.0 412.3 jit_solution(4510644713110703221)
XLA Ops:
  9.7 11.8 %all_gather.6 = bf16[1024,256]{1,0:T(8,128)(2,1)S(1)} all-gather(bf16[256,256]{1,0:T(8,128)(2,1)} %param.12), channel_id=1, replica_groups=mesh['row'=4,'col'=8] {'row'}, dimensions={0}, use_global_device_ids=true | all-gather | bytes 655360 | tf_op jit(solution)/shard_map/all_gather | solution.py:53
  21.8 119.2 %while.26 = (s32[]{:T(128)}, f32[16,128,256]{2,1,0:T(8,128)S(1)}, s32[256]{0:T(256)S(1)}, s32[256,16,128]{2,1,0:T(8,128)}, s32[]{:T(128)}, /*index=5*/s32[256]{0...) while((s32[]{:T(128)}, f32[16,128,256]{2,1,0:T(8,128)S(1)}, ...), condition=%wide.region_2.3_spmd, body=%wide.region_0.2_spmd.sunk | while | flops 271582656 | bytes 23862712 | solution.py:47
  25.7 4.5 %fusion.35 = f32[32,128,256]{2,1,0:T(8,128)} fusion(bf16[32,128,256]{2,1,0:T(8,128)(2,1)} %gather_fusion, s32[32]{0:T(128)S(1)} %and_convert_fusion.4, s32[128]{0:T(128)S(1)} %shift_right_arithmetic.118, s32[32,16,128]{2,1,0:T(8,128)S(1)} %constant_dynamic-slice_fusion.4), kind=kOutput, calls=%fused_computation.8.clone.1 | convolution fusion | flops 270532608 | bytes 6554240 | tf_op jit(solution)/shard_map/while/body/eval_jaxpr/bji,bjf->bif/dot_general | solution.py:36
  30.2 6.5 %scatter_fusion = f32[16,128,256]{2,1,0:T(8,128)S(1)} fusion(f32[16,128,256]{2,1,0:T(8,128)S(1)} %get-tuple-element.398, s32[32]{0:T(128)S(1)} %get-tuple-element.375, f32[32,128,256]{2,1,0:T(8,128)} %fusion.35), kind=kCustom, calls=%fused_computation.2.clone.1 | custom fusion | flops 1048576 | bytes 12583040 | tf_op jit(solution)/shard_map/while/body/eval_jaxpr/scatter-add | solution.py:43
  45.1 6.5 %scatter_fusion = f32[16,128,256]{2,1,0:T(8,128)S(1)} fusion(f32[16,128,256]{2,1,0:T(8,128)S(1)} %get-tuple-element.398, s32[32]{0:T(128)S(1)} %get-tuple-element.375, f32[32,128,256]{2,1,0:T(8,128)} %fusion.35), kind=kCustom, calls=%fused_computation.2.clone.1 | custom fusion | flops 1048576 | bytes 12583040 | tf_op jit(solution)/shard_map/while/body/eval_jaxpr/scatter-add | solution.py:43
  60.0 6.5 %scatter_fusion = f32[16,128,256]{2,1,0:T(8,128)S(1)} fusion(f32[16,128,256]{2,1,0:T(8,128)S(1)} %get-tuple-element.398, s32[32]{0:T(128)S(1)} %get-tuple-element.375, f32[32,128,256]{2,1,0:T(8,128)} %fusion.35), kind=kCustom, calls=%fused_computation.2.clone.1 | custom fusion | flops 1048576 | bytes 12583040 | tf_op jit(solution)/shard_map/while/body/eval_jaxpr/scatter-add | solution.py:43
  70.4 4.5 %fusion.35 = f32[32,128,256]{2,1,0:T(8,128)} fusion(bf16[32,128,256]{2,1,0:T(8,128)(2,1)} %gather_fusion, s32[32]{0:T(128)S(1)} %and_convert_fusion.4, s32[128]{0:T(128)S(1)} %shift_right_arithmetic.118, s32[32,16,128]{2,1,0:T(8,128)S(1)} %constant_dynamic-slice_fusion.4), kind=kOutput, calls=%fused_computation.8.clone.1 | convolution fusion | flops 270532608 | bytes 6554240 | tf_op jit(solution)/shard_map/while/body/eval_jaxpr/bji,bjf->bif/dot_general | solution.py:36
  74.9 6.5 %scatter_fusion = f32[16,128,256]{2,1,0:T(8,128)S(1)} fusion(f32[16,128,256]{2,1,0:T(8,128)S(1)} %get-tuple-element.398, s32[32]{0:T(128)S(1)} %get-tuple-element.375, f32[32,128,256]{2,1,0:T(8,128)} %fusion.35), kind=kCustom, calls=%fused_computation.2.clone.1 | custom fusion | flops 1048576 | bytes 12583040 | tf_op jit(solution)/shard_map/while/body/eval_jaxpr/scatter-add | solution.py:43
  89.8 6.5 %scatter_fusion = f32[16,128,256]{2,1,0:T(8,128)S(1)} fusion(f32[16,128,256]{2,1,0:T(8,128)S(1)} %get-tuple-element.398, s32[32]{0:T(128)S(1)} %get-tuple-element.375, f32[32,128,256]{2,1,0:T(8,128)} %fusion.35), kind=kCustom, calls=%fused_computation.2.clone.1 | custom fusion | flops 1048576 | bytes 12583040 | tf_op jit(solution)/shard_map/while/body/eval_jaxpr/scatter-add | solution.py:43
  104.7 6.5 %scatter_fusion = f32[16,128,256]{2,1,0:T(8,128)S(1)} fusion(f32[16,128,256]{2,1,0:T(8,128)S(1)} %get-tuple-element.398, s32[32]{0:T(128)S(1)} %get-tuple-element.375, f32[32,128,256]{2,1,0:T(8,128)} %fusion.35), kind=kCustom, calls=%fused_computation.2.clone.1 | custom fusion | flops 1048576 | bytes 12583040 | tf_op jit(solution)/shard_map/while/body/eval_jaxpr/scatter-add | solution.py:43
  119.6 6.5 %scatter_fusion = f32[16,128,256]{2,1,0:T(8,128)S(1)} fusion(f32[16,128,256]{2,1,0:T(8,128)S(1)} %get-tuple-element.398, s32[32]{0:T(128)S(1)} %get-tuple-element.375, f32[32,128,256]{2,1,0:T(8,128)} %fusion.35), kind=kCustom, calls=%fused_computation.2.clone.1 | custom fusion | flops 1048576 | bytes 12583040 | tf_op jit(solution)/shard_map/while/body/eval_jaxpr/scatter-add | solution.py:43
  129.9 4.5 %fusion.35 = f32[32,128,256]{2,1,0:T(8,128)} fusion(bf16[32,128,256]{2,1,0:T(8,128)(2,1)} %gather_fusion, s32[32]{0:T(128)S(1)} %and_convert_fusion.4, s32[128]{0:T(128)S(1)} %shift_right_arithmetic.118, s32[32,16,128]{2,1,0:T(8,128)S(1)} %constant_dynamic-slice_fusion.4), kind=kOutput, calls=%fused_computation.8.clone.1 | convolution fusion | flops 270532608 | bytes 6554240 | tf_op jit(solution)/shard_map/while/body/eval_jaxpr/bji,bjf->bif/dot_general | solution.py:36
  134.4 6.5 %scatter_fusion = f32[16,128,256]{2,1,0:T(8,128)S(1)} fusion(f32[16,128,256]{2,1,0:T(8,128)S(1)} %get-tuple-element.398, s32[32]{0:T(128)S(1)} %get-tuple-element.375, f32[32,128,256]{2,1,0:T(8,128)} %fusion.35), kind=kCustom, calls=%fused_computation.2.clone.1 | custom fusion | flops 1048576 | bytes 12583040 | tf_op jit(solution)/shard_map/while/body/eval_jaxpr/scatter-add | solution.py:43
  142.2 104.0 %while.27 = (s32[]{:T(128)}, f32[8,128,256]{2,1,0:T(8,128)S(1)}, s32[256]{0:T(256)S(1)}, s32[256,16,128]{2,1,0:T(8,128)}, s32[]{:T(128)}, /*index=5*/s32[256]{0:...) while((s32[]{:T(128)}, f32[8,128,256]{2,1,0:T(8,128)S(1)}, ...), condition=%wide.region_7.8_spmd, body=%wide.region_5.7_spmd.sunk | while | flops 271582656 | bytes 23862712 | solution.py:47
  148.8 6.5 %scatter_fusion.1 = f32[8,128,256]{2,1,0:T(8,128)S(1)} fusion(f32[8,128,256]{2,1,0:T(8,128)S(1)} %get-tuple-element.431, s32[32]{0:T(128)S(1)} %get-tuple-element.384, f32[32,128,256]{2,1,0:T(8,128)} %fusion.38), kind=kCustom, calls=%fused_computation.3.clone.1 | custom fusion | flops 1048576 | bytes 12583040 | tf_op jit(solution)/shard_map/while/body/eval_jaxpr/scatter-add | solution.py:43
  161.8 6.5 %scatter_fusion.1 = f32[8,128,256]{2,1,0:T(8,128)S(1)} fusion(f32[8,128,256]{2,1,0:T(8,128)S(1)} %get-tuple-element.431, s32[32]{0:T(128)S(1)} %get-tuple-element.384, f32[32,128,256]{2,1,0:T(8,128)} %fusion.38), kind=kCustom, calls=%fused_computation.3.clone.1 | custom fusion | flops 1048576 | bytes 12583040 | tf_op jit(solution)/shard_map/while/body/eval_jaxpr/scatter-add | solution.py:43
  174.8 6.5 %scatter_fusion.1 = f32[8,128,256]{2,1,0:T(8,128)S(1)} fusion(f32[8,128,256]{2,1,0:T(8,128)S(1)} %get-tuple-element.431, s32[32]{0:T(128)S(1)} %get-tuple-element.384, f32[32,128,256]{2,1,0:T(8,128)} %fusion.38), kind=kCustom, calls=%fused_computation.3.clone.1 | custom fusion | flops 1048576 | bytes 12583040 | tf_op jit(solution)/shard_map/while/body/eval_jaxpr/scatter-add | solution.py:43
  187.8 6.5 %scatter_fusion.1 = f32[8,128,256]{2,1,0:T(8,128)S(1)} fusion(f32[8,128,256]{2,1,0:T(8,128)S(1)} %get-tuple-element.431, s32[32]{0:T(128)S(1)} %get-tuple-element.384, f32[32,128,256]{2,1,0:T(8,128)} %fusion.38), kind=kCustom, calls=%fused_computation.3.clone.1 | custom fusion | flops 1048576 | bytes 12583040 | tf_op jit(solution)/shard_map/while/body/eval_jaxpr/scatter-add | solution.py:43
  200.8 6.5 %scatter_fusion.1 = f32[8,128,256]{2,1,0:T(8,128)S(1)} fusion(f32[8,128,256]{2,1,0:T(8,128)S(1)} %get-tuple-element.431, s32[32]{0:T(128)S(1)} %get-tuple-element.384, f32[32,128,256]{2,1,0:T(8,128)} %fusion.38), kind=kCustom, calls=%fused_computation.3.clone.1 | custom fusion | flops 1048576 | bytes 12583040 | tf_op jit(solution)/shard_map/while/body/eval_jaxpr/scatter-add | solution.py:43
  213.8 6.4 %scatter_fusion.1 = f32[8,128,256]{2,1,0:T(8,128)S(1)} fusion(f32[8,128,256]{2,1,0:T(8,128)S(1)} %get-tuple-element.431, s32[32]{0:T(128)S(1)} %get-tuple-element.384, f32[32,128,256]{2,1,0:T(8,128)} %fusion.38), kind=kCustom, calls=%fused_computation.3.clone.1 | custom fusion | flops 1048576 | bytes 12583040 | tf_op jit(solution)/shard_map/while/body/eval_jaxpr/scatter-add | solution.py:43
  226.8 6.4 %scatter_fusion.1 = f32[8,128,256]{2,1,0:T(8,128)S(1)} fusion(f32[8,128,256]{2,1,0:T(8,128)S(1)} %get-tuple-element.431, s32[32]{0:T(128)S(1)} %get-tuple-element.384, f32[32,128,256]{2,1,0:T(8,128)} %fusion.38), kind=kCustom, calls=%fused_computation.3.clone.1 | custom fusion | flops 1048576 | bytes 12583040 | tf_op jit(solution)/shard_map/while/body/eval_jaxpr/scatter-add | solution.py:43
  239.8 6.5 %scatter_fusion.1 = f32[8,128,256]{2,1,0:T(8,128)S(1)} fusion(f32[8,128,256]{2,1,0:T(8,128)S(1)} %get-tuple-element.431, s32[32]{0:T(128)S(1)} %get-tuple-element.384, f32[32,128,256]{2,1,0:T(8,128)} %fusion.38), kind=kCustom, calls=%fused_computation.3.clone.1 | custom fusion | flops 1048576 | bytes 12583040 | tf_op jit(solution)/shard_map/while/body/eval_jaxpr/scatter-add | solution.py:43
  250.9 21.3 %reduce-scatter.5.cloned.1.call-done = bf16[256,256]{1,0:T(8,128)(2,1)} async-done(((bf16[1024,256]{1,0:T(8,128)(2,1)}), bf16[256,256]{1,0:T(8,128)(2,1)}) %reduce-scatter.5.cloned.1.call-update) | async-done | bytes 131088 | tf_op jit(solution)/shard_map/reduce_scatter | solution.py:78
  274.1 130.1 %all-reduce.2.cloned.1.call-done = f32[256,256]{1,0:T(8,128)} async-done(((f32[256,256]{1,0:T(8,128)}), f32[256,256]{1,0:T(8,128)}) %all-reduce.2.cloned.1.call-update) | async-done | bytes 262160 | tf_op jit(solution)/shard_map/psum | solution.py:99
  (153 shorter events, 117.5 us)
Async XLA Ops:
  7.2 242.0 %copy-start = (bf16[256,256]{1,0:T(8,128)(2,1)S(1)}, bf16[256,256]{1,0:T(8,128)(2,1)}, u32[]{:S(2)}) copy-start(bf16[256,256]{1,0:T(8,128)(2,1)} %param.15) | copy-start | bytes 393220
  7.2 14.6 %copy-start.2 = (s32[1,1,256]{2,1,0:T(1,128)S(1)}, s32[1,1,256]{2,1,0:T(1,128)}, u32[]{:S(2)}) copy-start(s32[1,1,256]{2,1,0:T(1,128)} %param.16) | copy-start | bytes 3076
  7.2 14.6 %copy-start.3 = (s32[1,1,256]{2,1,0:T(1,128)S(1)}, s32[1,1,256]{2,1,0:T(1,128)}, u32[]{:S(2)}) copy-start(s32[1,1,256]{2,1,0:T(1,128)} %param.17) | copy-start | bytes 3076
  7.2 134.9 %all-gather.2.cloned.1.call-start = ((), (), s32[]{:S(2)}) async-start(), calls=%async_computation.4 | async-start | bytes 1179648 | tf_op jit(solution)/shard_map/all_gather | solution.py:74
  9.7 237.5 %reduce-scatter.3.cloned.1.call-start = ((), (), s32[]{:S(2)}) async-start(), calls=%async_computation.2 | async-start | bytes 1179648 | tf_op jit(solution)/shard_map/reduce_scatter | solution.py:57
  142.1 130.2 %reduce-scatter.5.cloned.1.call-start = ((), (), s32[]{:S(2)}) async-start(), calls=%async_computation.5 | async-start | bytes 655360 | tf_op jit(solution)/shard_map/reduce_scatter | solution.py:78
  246.2 1.0 copy-start.1
  247.1 157.0 %all-reduce.2.cloned.1.call-start = ((), (), s32[]{:S(2)}) async-start(), calls=%async_computation.3 | async-start | bytes 524288 | tf_op jit(solution)/shard_map/psum | solution.py:99
Sparse Core Ops, SparseCore 0:
  10.2 24.8 all-gather.1
  142.2 32.5 reduce-scatter.2
  247.2 25.0 reduce-scatter.4
  279.1 124.9 all-reduce.1
where the time goes:
time: 415 us; the launch traced here: 412 us
  waiting for transfers between devices  152 us (37%)
  other arithmetic  121 us (29%)
  matrix products  63.2 us (15%)
  local copies, waits for them, and re-layouts  50.3 us (12%)
  between operations  13.9 us (3%)
  blocking collectives  11.8 us (3%)
    psum x1, waiting for transfers between devices, per_device(): weight_grad = lax.psum(local_term, ('row', 'col'))  130 us
    scatter-add x16, other arithmetic, one_block(): return totals.at[placed].add(product)  104 us
    dot_general x8, matrix products, one_block(): jnp.einsum('bji,bjf->bif', pattern, source[block_cols], preferred_element...  36 us
    dot_general x8, matrix products, one_block(): jnp.einsum('bji,bif->bjf', pattern, source[block_rows], preferred_element...  21.7 us
    reduce_scatter x1, waiting for transfers between devices, backward_pass(): lax.psum_scatter(partial_value.reshape(-1, width).astype(jnp.bfloat16), '...  21.3 us
    gather x8, local copies, waits for them, and re-layouts, one_block(): source[block_cols]  16 us
    dynamic_slice x16, local copies, waits for them, and re-layouts, one_block(): block_bits = lax.dynamic_slice_in_dim(packed, offset, block_size, 0)  15.6 us
    gather x8, local copies, waits for them, and re-layouts, one_block(): source[block_rows]  15.3 us
  transfers between devices with their start and end apart: 4, of which 2 were waited for; matrix products, arithmetic and copies ran while one was open for 56% of the time, Pallas kernels for 0%

commit v1 on v0

v1 whole, which is shorter than its diff:
```python
import functools

import jax
import jax.numpy as jnp
from jax import lax
from jax.experimental import pallas as pl
from jax.experimental.pallas import tpu as pltpu
from jax.sharding import PartitionSpec as P

SMEM = pltpu.SMEM
VMEM = pltpu.VMEM
BF16 = jnp.bfloat16
F32 = jnp.float32


def build_kernel(trows, chunk, count_ref, rows_ref, cols_ref, bits_ref, out_ref, acc0, acc1):
    base = pl.program_id(0) * chunk
    zero = jnp.zeros(acc0.shape[1:], jnp.int32)

    def clear(p, carry):
        acc0[p] = zero
        acc1[p] = zero
        return carry

    lax.fori_loop(0, chunk * trows, clear, 0, unroll=4)
    count = count_ref[0]

    def add_pair(k, carry):
        for half, acc in enumerate((acc0, acc1)):
            s = 2 * k + half
            col = cols_ref[s] - base
            ok = (s < count) & (col >= 0) & (col < chunk)
            p = jnp.where(ok, col * trows + rows_ref[s], 0)
            words = bits_ref[s]
            word = (words[:8] | (words[8:] << 16)) & (0 - ok.astype(jnp.int32))
            for b in range(8):
                acc[p, b] += (word >> b) & 0x10001
        return carry

    lax.fori_loop(0, (count + 1) // 2, add_pair, 0)

    def convert(row, carry):
        lanes = pl.ds(pl.multiple_of(row * 128, 128), 128)
        for col in range(chunk):
            p = col * trows + row
            for b in range(8):
                v = acc0[p, b] + acc1[p, b]
                both = jnp.concatenate([v & 0xFFFF, v >> 16], axis=0)
                out_ref[pl.ds(col * 128 + b * 16, 16), lanes] = both.astype(F32).astype(BF16)
        return carry

    lax.fori_loop(0, trows, convert, 0)


def build_adjacency(count, rows, cols, bits, trows, tcols):
    chunk = max(d for d in range(1, tcols + 1) if tcols % d == 0 and d * trows <= 128)
    scratch = pltpu.VMEM((chunk * trows, 8, 8, 128), jnp.int32)
    return pl.pallas_call(
        functools.partial(build_kernel, trows, chunk),
        grid=(tcols // chunk,),
        out_shape=jax.ShapeDtypeStruct((tcols * 128, trows * 128), BF16),
        in_specs=[
            pl.BlockSpec(memory_space=SMEM),
            pl.BlockSpec(memory_space=SMEM),
            pl.BlockSpec(memory_space=SMEM),
            pl.BlockSpec(memory_space=VMEM),
        ],
        out_specs=pl.BlockSpec((chunk * 128, trows * 128), lambda g: (g, 0)),
        scratch_shapes=[scratch, scratch],
        compiler_params=pltpu.CompilerParams(vmem_limit_bytes=40 * 2**20),
        name="build_adjacency",
    )(count, rows, cols, bits)


def swap_order(x, a, b):
    return x.reshape(-1, a, b, x.shape[-1]).swapaxes(1, 2).reshape(x.shape)


def per_device(features, cotangent, degrees, weight, tile_rows, tile_cols, tile_bits, tile_count):
    nodes, width = features.shape
    trows = nodes * lax.axis_size("col") // 128
    tcols = nodes * lax.axis_size("row") // 128
    at = build_adjacency(
        tile_count[0], tile_rows[0, 0], tile_cols[0, 0], tile_bits[0, 0], trows, tcols
    )
    deg = degrees[:, None].astype(F32)
    scaled = (cotangent.astype(F32) / deg).astype(BF16)
    feats = lax.all_gather(swap_order(features, 16, 8), "row", axis=0, tiled=True)
    grads = lax.all_gather(scaled, "col", axis=0, tiled=True)
    fwd = lax.dot_general(at, feats, (((0,), (0,)), ((), ())), preferred_element_type=F32)
    fwd = fwd.astype(BF16)
    local = lax.dot_general(fwd, grads, (((0,), (0,)), ((), ())), preferred_element_type=F32)
    weight_grad = lax.psum(local, ("row", "col"))
    summed = lax.psum_scatter(fwd, "col", scatter_dimension=0, tiled=True).astype(F32)
    aggregated = (summed / deg).astype(BF16)
    output = jnp.dot(aggregated, weight, preferred_element_type=F32).astype(BF16)
    bwd = jnp.dot(at, grads, preferred_element_type=F32).astype(BF16)
    back = swap_order(lax.psum_scatter(bwd, "row", scatter_dimension=0, tiled=True), 8, 16)
    input_grad = jnp.dot(back, weight.T, preferred_element_type=F32).astype(BF16)
    return output, weight_grad, input_grad


def solution(mesh):
    placed = (
        P(("col", "row"), None),
        P(("row", "col"), None),
        P(("row", "col")),
        P(),
        P("row", "col", None),
        P("row", "col", None),
        P("row", "col", None, None, None),
        P("row", "col"),
    )
    return jax.shard_map(
        per_device,
        mesh=mesh,
        in_specs=placed,
        out_specs=(P(("row", "col"), None), P(), P(("col", "row"), None)),
        check_vma=False,
    )
```

time: 415 us -> 236 us (0.57)
  other arithmetic: 121 us -> 2.38 us
  matrix products: 63.2 us -> 10.9 us
  local copies, waits for them, and re-layouts: 50.3 us -> 6.51 us
  waiting for transfers between devices: 152 us -> 184 us
  Pallas kernels: 0 us -> 5.02 us
    scatter-add x16 -> x0, other arithmetic: 104 us -> none  [one_block(): return totals.at[placed].add(product)]
    dot_general x19 -> x5, matrix products: 63.2 us -> 10.9 us  [the longest x1 4.64 us: per_device(): bwd = jnp.dot(at, grads, preferred_element_type=F32).astype(BF16)]
    gather x16 -> x0, local copies, waits for them, and re-layouts: 31.3 us -> none  [the longest x8 16 us: one_block(): source[block_cols]]
    reduce_scatter x2, waiting for transfers between devices: 21.4 us -> 52.4 us  [the longest x1 28.4 us: per_device(): lax.psum_scatter(fwd, 'col', scatter_dimension=0, tiled=True).astype(F32)]
    dynamic_slice x16 -> x0, local copies, waits for them, and re-layouts: 15.6 us -> none  [one_block(): block_bits = lax.dynamic_slice_in_dim(packed, offset, block_size, 0)]
    convert_element_type x20 -> x2, other arithmetic: 15.9 us -> 2.38 us  [the longest x1 1.67 us: per_device(): scaled = (cotangent.astype(F32) / deg).astype(BF16)]
    pallas_call x0 -> x1, Pallas kernels: none -> 5.02 us  [build_adjacency(): pl.pallas_call(functools.partial(build_kernel, trows, chunk), grid=(tcols...]
  transfers between devices with their start and end apart: 4 -> 4, of which waited for: 2 -> 4; matrix products, arithmetic and copies ran while one was open for 56% -> 5% of each run, Pallas kernels for 0% -> 2%
where the time goes in v1:
time: 236 us; the launch traced here: 235 us
  waiting for transfers between devices  184 us (78%)
  between operations  14.5 us (6%)
  blocking collectives  11.5 us (5%)
  matrix products  10.9 us (5%)
  local copies, waits for them, and re-layouts  6.51 us (3%)
  Pallas kernels  5.02 us (2%)
  other arithmetic  2.38 us (1%)
    psum x1, waiting for transfers between devices, per_device(): weight_grad = lax.psum(local, ('row', 'col'))  130 us
    reduce_scatter x1, waiting for transfers between devices, per_device(): lax.psum_scatter(fwd, 'col', scatter_dimension=0, tiled=True).astype(F32)  28.4 us
    reduce_scatter x1, waiting for transfers between devices, per_device(): lax.psum_scatter(bwd, 'row', scatter_dimension=0, tiled=True)  24 us
    all_gather x1, blocking collectives, per_device(): lax.all_gather(swap_order(features, 16, 8), 'row', axis=0, tiled=True)  11.5 us
    pallas_call x1, Pallas kernels, build_adjacency(): pl.pallas_call(functools.partial(build_kernel, trows, chunk), grid=(tcols...  5.02 us
  transfers between devices with their start and end apart: 4, of which 4 were waited for; matrix products, arithmetic and copies ran while one was open for 5% of the time, Pallas kernels for 2%

profile of v1, /device:TPU:0, one launch (start us, length us, event | category | flops | bytes accessed | tf_op | source)
XLA Modules:
  0.0 235.2 jit_solution(18355046354589894693)
XLA Ops:
  7.2 0.0 all-gather.2.cloned.1.call-start
  7.2 0.7 convert_element_type.30
  7.9 1.7 divide_convert_fusion
  9.6 0.0 reduce-scatter.3.cloned.1.call-start
  10.3 0.9 copy.12
  11.3 1.6 copy-done.2
  12.9 0.7 copy-done.3
  13.5 0.7 copy-done.4
  14.2 5.0 %build_adjacency.1 = bf16[1024,2048]{1,0:T(8,128)(2,1)S(1)} custom-call(s32[1]{0:T(128)} %bitcast.21.count_ref, s32[256]{0:T(256)S(1)} %bitcast.23, s32[256]{0:T(256)S(1)} %bitcast.24, s32[256,16,128]{2,1,0:T(8,128)S(1)} %bitcast.22), custom_call_target="tpu_custom_call" | custom-call | tf_op jit(solution)/shard_map/build_adjacency/pallas_call | solution.py:58
  19.2 11.5 %all_gather.6 = bf16[1024,256]{1,0:T(8,128)(2,1)S(1)} all-gather(bf16[256,256]{1,0:T(8,128)(2,1)S(1)} %bitcast.25), channel_id=1, replica_groups=mesh['row'=4,'col'=8] {'row'}, dimensions={0}, use_global_device_ids=true | all-gather | bytes 655360 | tf_op jit(solution)/shard_map/all_gather | solution.py:88
  30.7 2.4 %convolution_convert_fusion = bf16[2048,256]{1,0:T(8,128)(2,1)} fusion(bf16[1024,2048]{1,0:T(8,128)(2,1)S(1)} %build_adjacency.1, bf16[1024,256]{1,0:T(8,128)(2,1)S(1)} %all_gather.6), kind=kOutput, calls=%fused_computation | convolution fusion | flops 1074266112 | bytes 5767168 | tf_op jit(solution)/shard_map/dot_general | solution.py:90
  33.2 0.0 reduce-scatter.5.cloned.1.call-start
  33.2 1.8 all-gather.2.cloned.1.call-done
  35.0 4.6 %convolution_convert_fusion.1 = bf16[1024,256]{1,0:T(8,128)(2,1)} fusion(bf16[1024,2048]{1,0:T(8,128)(2,1)} %copy-done.1, bf16[2048,256]{1,0:T(8,128)(2,1)} %all-gather.2.cloned.1.call-done), kind=kOutput, calls=%fused_computation.1 | convolution fusion | flops 1074003968 | bytes 5767168 | tf_op jit(solution)/shard_map/dot_general | solution.py:97
  39.7 0.0 reduce-scatter.5.cloned.1.call-update
  39.7 0.0 all-reduce.2.cloned.1.call-start
  39.8 1.2 fusion.1
  41.0 28.4 %reduce-scatter.3.cloned.1.call-done = bf16[256,256]{1,0:T(8,128)(2,1)} async-done(((bf16[2048,256]{1,0:T(8,128)(2,1)}), bf16[256,256]{1,0:T(8,128)(2,1)}) %reduce-scatter.3.cloned.1.call-update) | async-done | bytes 131088 | tf_op jit(solution)/shard_map/reduce_scatter | solution.py:94
  69.4 1.8 convolution_convert_fusion.3
  71.2 24.0 %reduce-scatter.5.cloned.1.call-done = bf16[256,256]{1,0:T(8,128)(2,1)} async-done(((bf16[1024,256]{1,0:T(8,128)(2,1)}), bf16[256,256]{1,0:T(8,128)(2,1)}) %reduce-scatter.5.cloned.1.call-update) | async-done | bytes 131088 | tf_op jit(solution)/shard_map/reduce_scatter | solution.py:98
  95.2 0.9 copy.13
  96.2 0.9 convolution_convert_fusion.2
  97.0 130.0 %all-reduce.2.cloned.1.call-done = f32[256,256]{1,0:T(8,128)} async-done(((f32[256,256]{1,0:T(8,128)}), f32[256,256]{1,0:T(8,128)}) %all-reduce.2.cloned.1.call-update) | async-done | bytes 262160 | tf_op jit(solution)/shard_map/psum | solution.py:93
  227.0 1.7 copy.16
  (14 shorter events, 0.1 us)
Async XLA Ops:
  7.2 62.2 %copy-start = (bf16[256,256]{1,0:T(8,128)(2,1)S(1)}, bf16[256,256]{1,0:T(8,128)(2,1)}, u32[]{:S(2)}) copy-start(bf16[256,256]{1,0:T(8,128)(2,1)} %param.11) | copy-start | bytes 393220
  7.2 27.8 %all-gather.2.cloned.1.call-start = ((), (), s32[]{:S(2)}) async-start(), calls=%async_computation.3 | async-start | bytes 1179648 | tf_op jit(solution)/shard_map/all_gather | solution.py:89
  9.6 59.8 %reduce-scatter.3.cloned.1.call-start = ((), (), s32[]{:S(2)}) async-start(), calls=%async_computation.2 | async-start | bytes 1179648 | tf_op jit(solution)/shard_map/reduce_scatter | solution.py:94
  11.3 1.6 copy-start.2
  12.9 0.7 copy-start.3
  13.5 0.7 copy-start.4
  19.2 11.5 %copy-start.1 = (bf16[1024,2048]{1,0:T(8,128)(2,1)}, bf16[1024,2048]{1,0:T(8,128)(2,1)S(1)}, u32[]{:S(2)}) copy-start(bf16[1024,2048]{1,0:T(8,128)(2,1)S(1)} %build_adjacency.1) | copy-start | bytes 12582916
  33.2 6.6 %copy-start.5 = (bf16[2048,256]{1,0:T(8,128)(2,1)S(1)}, bf16[2048,256]{1,0:T(8,128)(2,1)}, u32[]{:S(2)}) copy-start(bf16[2048,256]{1,0:T(8,128)(2,1)} %convolution_convert_fusion) | copy-start | bytes 3145732
  33.2 62.0 %reduce-scatter.5.cloned.1.call-start = ((), (), s32[]{:S(2)}) async-start(), calls=%async_computation.5 | async-start | bytes 655360 | tf_op jit(solution)/shard_map/reduce_scatter | solution.py:98
  35.0 4.7 %copy-start.6 = (bf16[2048,256]{1,0:T(8,128)(2,1)S(1)}, bf16[2048,256]{1,0:T(8,128)(2,1)}, u32[]{:S(2)}) copy-start(bf16[2048,256]{1,0:T(8,128)(2,1)} %all-gather.2.cloned.1.call-done) | copy-start | bytes 3145732
  39.7 187.3 %all-reduce.2.cloned.1.call-start = ((), (), s32[]{:S(2)}) async-start(), calls=%async_computation.4 | async-start | bytes 524288 | tf_op jit(solution)/shard_map/psum | solution.py:93
Sparse Core Ops, SparseCore 0:
  10.2 24.7 all-gather.1
  37.3 32.0 reduce-scatter.2
  72.2 22.9 reduce-scatter.4
  102.0 124.9 all-reduce.1

commit v2 on v1

--- a/solution.py
+++ b/solution.py
@@ -72,6 +72,241 @@
     )(count, rows, cols, bits)
 
 
+MESH = pl.DeviceIdType.MESH
+
+
+def copy_to(src, dst, send_sem, recv_sem, device):
+    return pltpu.make_async_remote_copy(
+        src_ref=src,
+        dst_ref=dst,
+        send_sem=send_sem,
+        recv_sem=recv_sem,
+        device_id=device,
+        device_id_type=MESH,
+    )
+
+
+def dot(a, b, dims=((1,), (0,))):
+    return lax.dot_general(a, b, (dims, ((), ())), preferred_element_type=F32)
+
+
+def layer_kernel(
+    n_row, n_z,
+    at_ref, feat_ref, cot_ref, deg_ref, weight_ref,
+    out_ref, wgrad_ref, igrad_ref,
+    feats, grads, part, pair, sums, arrived, back, back_in, w_part, w_in, w_all,
+    feat_s, feat_r, grad_s, grad_r, relay_s, pair_s, pair_r, sum_s, sum_r, back_s, back_r,
+    w1_s, w1_r, w2_s, w2_r,
+):
+    n = feat_ref.shape[0]
+    n_col = 2 * n_z
+    n_all = n_row * n_col
+    r = lax.axis_index("row")
+    c = lax.axis_index("col")
+    me = r * n_col + c
+    z = c // 2
+    core = c % 2
+    sibling = (r, z * 2 + 1 - core)
+
+    def peer_of(i):
+        peer = (me + i) % n_all
+        return peer, (peer // n_col, peer % n_col)
+
+    barrier = pltpu.get_barrier_semaphore()
+
+    @pl.loop(1, n_all)
+    def _(i):
+        pl.semaphore_signal(barrier, inc=1, device_id=peer_of(i)[1], device_id_type=MESH)
+
+    i0 = lax.broadcasted_iota(jnp.int32, (n, n), 0)
+    i1 = lax.broadcasted_iota(jnp.int32, (n, n), 1)
+    placed = (i1 // 128) * 128 + (i1 % 16) * 8 + (i1 % 128) // 16
+    order = (i0 == placed).astype(F32).astype(BF16)
+    deg_row = deg_ref[...].astype(F32)
+    deg_col = jnp.sum(jnp.where(i0 == i1, deg_row, 0.0), axis=1, keepdims=True)
+    grads[c] = (cot_ref[...].astype(F32) / deg_col).astype(BF16)
+    feats[r] = dot(feat_ref[...], order, ((0,), (0,))).astype(BF16)
+
+    pl.semaphore_wait(barrier, n_all - 1)
+
+    def feat_copy(i):
+        q = (r + i) % n_row
+        return q, copy_to(feats.at[r], feats.at[r], feat_s.at[q], feat_r.at[r], (q, c))
+
+    def grad_copy(i):
+        q = ((z + i) % n_z) * 2 + core
+        return q, copy_to(grads.at[c], grads.at[c], grad_s.at[q], grad_r.at[c], (r, q))
+
+    def relay_copy(q):
+        return copy_to(grads.at[q], grads.at[q], relay_s.at[q // 2], grad_r.at[q], sibling)
+
+    for i in range(1, n_row):
+        feat_copy(i)[1].start()
+    for i in range(1, n_z):
+        grad_copy(i)[1].start()
+    relay_copy(c).start()
+
+    def arrive(ref, sem, slot):
+        copy_to(ref.at[slot], ref.at[slot], sem.at[slot], sem.at[slot], sibling).wait_recv()
+
+    for i in range(1, n_row):
+        arrive(feats, feat_r, (r + i) % n_row)
+
+    def forward(q):
+        lanes = pl.ds(pl.multiple_of(q * n, n), n)
+        total = dot(feats[0], at_ref[pl.ds(0, n), lanes])
+        for k in range(1, n_row):
+            total += dot(feats[k], at_ref[pl.ds(k * n, n), lanes])
+        part[q] = total.astype(BF16)
+
+    def pair_copy(zz):
+        q = zz * 2 + 1 - core
+        return copy_to(part.at[q], pair.at[zz], pair_s.at[zz], pair_r.at[zz], sibling)
+
+    @pl.loop(1, n_z + 1)
+    def _(i):
+        zz = (z + i) % n_z
+        forward(zz * 2 + 1 - core)
+        pair_copy(zz).start()
+
+    @pl.loop(1, n_z + 1)
+    def _(i):
+        forward(((z + i) % n_z) * 2 + core)
+
+    def sum_copy(i):
+        zz = (z + i) % n_z
+        return copy_to(
+            sums.at[zz], arrived.at[z], sum_s.at[zz], sum_r.at[z], (r, zz * 2 + core)
+        )
+
+    @pl.loop(1, n_z)
+    def _(i):
+        zz = (z + i) % n_z
+        arrive(pair, pair_r, zz)
+        sums[zz] = (part[zz * 2 + core].astype(F32) + pair[zz].astype(F32)).astype(BF16)
+        sum_copy(i).start()
+
+    for i in range(1, n_z):
+        q = ((z + i) % n_z) * 2 + core
+        arrive(grads, grad_r, q)
+        relay_copy(q).start()
+    for i in range(n_z):
+        arrive(grads, grad_r, ((z + i) % n_z) * 2 + 1 - core)
+
+    def back_copy(q):
+        return copy_to(back.at[q], back_in.at[r], back_s.at[q], back_r.at[r], (q, c))
+
+    def backward(q):
+        rows = pl.ds(pl.multiple_of(q * n, n), n)
+        back[q] = dot(at_ref[rows, :], grads[...].reshape(n_col * n, -1)).astype(BF16)
+
+    @pl.loop(1, n_row)
+    def _(i):
+        q = (r + i) % n_row
+        backward(q)
+        back_copy(q).start()
+
+    local = dot(part[0], grads[0])
+    for q in range(1, n_col):
+        local += dot(part[q], grads[q])
+    blocks = [(pl.ds((d // 2) * 16, 16), pl.ds((d % 2) * 128, 128)) for d in range(n_all)]
+    rounded = local.astype(BF16)
+    for d in range(n_all):
+        top, left = (d // 2) * 16, (d % 2) * 128
+        w_part[d] = rounded[top : top + 16, left : left + 128]
+
+    def w1_copy(i):
+        peer, device = peer_of(i)
+        return copy_to(w_part.at[peer], w_in.at[me], w1_s.at[peer], w1_r.at[me], device)
+
+    def w2_copy(i):
+        peer, device = peer_of(i)
+        return copy_to(w_all.at[me], w_all.at[me], w2_s.at[peer], w2_r.at[me], device)
+
+    @pl.loop(1, n_all)
+    def _(i):
+        w1_copy(i).start()
+
+    backward(r)
+    w_in[me] = w_part[me]
+
+    @pl.loop(1, n_all)
+    def _(i):
+        arrive(w_in, w1_r, (me + i) % n_all)
+
+    w_all[me] = jnp.sum(w_in[...].astype(F32), axis=0).astype(BF16)
+
+    @pl.loop(1, n_all)
+    def _(i):
+        w2_copy(i).start()
+
+    arrive(pair, pair_r, z)
+    total = part[c].astype(F32) + pair[z].astype(F32)
+    for i in range(1, n_z):
+        zz = (z + i) % n_z
+        arrive(arrived, sum_r, zz)
+        total += arrived[zz].astype(F32)
+    out_ref[...] = dot((total / deg_row).astype(BF16), weight_ref[...], ((0,), (0,))).astype(BF16)
+
+    total = back[r].astype(F32)
+    for i in range(1, n_row):
+        q = (r + i) % n_row
+        arrive(back_in, back_r, q)
+        total += back_in[q].astype(F32)
+    ordered = dot(order, total.astype(BF16)).astype(BF16)
+    igrad_ref[...] = dot(ordered, weight_ref[...], ((1,), (1,))).astype(BF16)
+
+    @pl.loop(1, n_all)
+    def _(i):
+        arrive(w_all, w2_r, (me + i) % n_all)
+
+    for d in range(n_all):
+        wgrad_ref[blocks[d]] = w_all[d].astype(F32)
+
+    for i in range(1, n_row):
+        feat_copy(i)[1].wait_send()
+        back_copy((r + i) % n_row).wait_send()
+    for i in range(1, n_z):
+        grad_copy(i)[1].wait_send()
+        sum_copy(i).wait_send()
+    for i in range(n_z):
+        zz = (z + i) % n_z
+        relay_copy(zz * 2 + core).wait_send()
+        pair_copy(zz).wait_send()
+
+    @pl.loop(1, n_all)
+    def _(i):
+        w1_copy(i).wait_send()
+        w2_copy(i).wait_send()
+
+
+def layer(at, features, cotangent, degrees, weight, n_row, n_z):
+    n, width = features.shape
+    n_col = 2 * n_z
+    n_all = n_row * n_col
+    block = lambda k: pltpu.VMEM((k, n, width), BF16)
+    sems = lambda k: pltpu.SemaphoreType.DMA((k,))
+    small = pltpu.VMEM((n_all, 16, 128), BF16)
+    tile = jax.ShapeDtypeStruct((n, width), BF16)
+    return pl.pallas_call(
+        functools.partial(layer_kernel, n_row, n_z),
+        out_shape=(tile, jax.ShapeDtypeStruct((width, width), F32), tile),
+        in_specs=[pl.BlockSpec(memory_space=VMEM)] * 5,
+        out_specs=(pl.BlockSpec(memory_space=VMEM),) * 3,
+        scratch_shapes=[
+            block(n_row), block(n_col), block(n_col), block(n_z), block(n_z), block(n_z),
+            block(n_row), block(n_row), small, small, small,
+            sems(n_row), sems(n_row), sems(n_col), sems(n_col), sems(n_z), sems(n_z), sems(n_z),
+            sems(n_z), sems(n_z), sems(n_row), sems(n_row),
+            sems(n_all), sems(n_all), sems(n_all), sems(n_all),
+        ],
+        compiler_params=pltpu.CompilerParams(
+            collective_id=0, has_side_effects=True, vmem_limit_bytes=48 * 2**20
+        ),
+        name="layer",
+    )(at, features, cotangent, degrees, weight)
+
+
 def swap_order(x, a, b):
     return x.reshape(-1, a, b, x.shape[-1]).swapaxes(1, 2).reshape(x.shape)
 
@@ -83,6 +318,11 @@
     at = build_adjacency(
         tile_count[0], tile_rows[0, 0], tile_cols[0, 0], tile_bits[0, 0], trows, tcols
     )
+    n_row, n_col = lax.axis_size("row"), lax.axis_size("col")
+    if n_row * n_col * 16 * 128 == width * width and nodes == width:
+        return layer(
+            at, features, cotangent, degrees.reshape(1, nodes), weight, n_row, n_col // 2
+        )
     deg = degrees[:, None].astype(F32)
     scaled = (cotangent.astype(F32) / deg).astype(BF16)
     feats = lax.all_gather(swap_order(features, 16, 8), "row", axis=0, tiled=True)

time: 236 us -> 53.8 us (0.23)
  waiting for transfers between devices: 184 us -> 0 us
  Pallas kernels: 5.02 us -> 47.4 us
  between operations: 14.5 us -> 1.36 us
  blocking collectives: 11.5 us -> 0 us
  matrix products: 10.9 us -> 0 us
  other arithmetic: 2.38 us -> 0 us
    psum x1 -> x0, waiting for transfers between devices: 130 us -> none  [per_device(): weight_grad = lax.psum(local, ('row', 'col'))]
    reduce_scatter x2 -> x0, waiting for transfers between devices: 52.4 us -> none  [the longest x1 28.4 us: per_device(): lax.psum_scatter(fwd, 'col', scatter_dimension=0, tiled=True).astype(F32)]
    pallas_call x0 -> x1, Pallas kernels: none -> 44.2 us  [layer(): pl.pallas_call(functools.partial(layer_kernel, n_row, n_z), out_shape=(ti...]
    all_gather x1 -> x0, blocking collectives: 11.5 us -> none  [per_device(): lax.all_gather(swap_order(features, 16, 8), 'row', axis=0, tiled=True)]
    dot_general x5 -> x0, matrix products: 10.9 us -> none  [the longest x1 4.64 us: per_device(): bwd = jnp.dot(at, grads, preferred_element_type=F32).astype(BF16)]
    convert_element_type x2 -> x0, other arithmetic: 2.38 us -> none  [the longest x1 1.67 us: per_device(): scaled = (cotangent.astype(F32) / deg).astype(BF16)]
    unnamed x15 -> x17, local copies, waits for them, and re-layouts: 4.63 us -> 4.97 us
  transfers between devices with their start and end apart: 4 -> 0, of which waited for: 4 -> 0; matrix products, arithmetic and copies ran while one was open for 5% -> 0% of each run, Pallas kernels for 2% -> 0%
where the time goes in v2:
time: 53.8 us
  Pallas kernels  47.4 us (88%)
  local copies, waits for them, and re-layouts  4.97 us (9%)
  between operations  1.36 us (3%)
    pallas_call x1, Pallas kernels, layer(): pl.pallas_call(functools.partial(layer_kernel, n_row, n_z), out_shape=(ti...  44.2 us
    unnamed x17, local copies, waits for them, and re-layouts  4.97 us
    pallas_call x1, Pallas kernels, build_adjacency(): pl.pallas_call(functools.partial(build_kernel, trows, chunk), grid=(tcols...  3.27 us

profile of v2, /device:TPU:0, one launch (start us, length us, event | category | flops | bytes accessed | tf_op | source)
XLA Modules:
  0.0 53.8 jit_solution(7827451124522491399)
XLA Ops:
  0.6 0.0 copy-start.6
  1.3 0.0 copy-start
  1.3 1.6 %copy-done = s32[1,1,256,16,128]{4,3,2,1,0:T(8,128)S(1)} copy-done((s32[1,1,256,16,128]{4,3,2,1,0:T(8,128)S(1)}, s32[1,1,256,16,128]{4,3,2,1,0:T(8,128)}, u32[]{:S(2)}) %copy-start) | copy-done | bytes 2097176
  2.9 0.0 copy-start.4
  2.9 0.7 %copy-done.4 = s32[1,1,256]{2,1,0:T(1,128)S(1)} copy-done((s32[1,1,256]{2,1,0:T(1,128)S(1)}, s32[1,1,256]{2,1,0:T(1,128)}, u32[]{:S(2)}) %copy-start.4) | copy-done | bytes 1048
  3.6 0.0 copy-start.5
  3.6 0.7 %copy-done.5 = s32[1,1,256]{2,1,0:T(1,128)S(1)} copy-done((s32[1,1,256]{2,1,0:T(1,128)S(1)}, s32[1,1,256]{2,1,0:T(1,128)}, u32[]{:S(2)}) %copy-start.5) | copy-done | bytes 1048
  4.3 0.0 copy-start.1
  4.3 0.0 copy-start.2
  4.3 0.0 copy-start.3
  4.3 3.3 %build_adjacency.1.at_ref = bf16[1024,2048]{1,0:T(8,128)(2,1)S(1)} custom-call(s32[1]{0:T(128)} %bitcast.5.count_ref, s32[256]{0:T(256)S(1)} %bitcast.7, s32[256]{0:T(256)S(1)} %bitcast.8, s32[256,16,128]{2,1,0:T(8,128)S(1)} %bitcast.6), custom_call_target="tpu_custom_call" | custom-call | tf_op jit(solution)/shard_map/build_adjacency/pallas_call | solution.py:58
  7.5 0.0 copy-done.6
  7.5 0.0 copy-done.1
  7.6 0.0 copy-done.2
  7.6 0.0 copy-done.3
  7.6 44.2 %layer.1 = (bf16[256,256]{1,0:T(8,128)(2,1)S(1)}, f32[256,256]{1,0:T(8,128)S(1)}, bf16[256,256]{1,0:T(8,128)(2,1)S(1)}) custom-call(bf16[1024,2048]{1,0:T(8,128)(2,1)S(1)} %build_adjacency.1.at_ref, bf16[256,256]{1,0:T(8,128)(2,1)S(1)} %copy-done.1, bf16[256,256]{1,0:T(8,128)(2,1)S(1)} %copy-done.2, s32[1,256]{1,0:T(1,128)S(1)} %bitcast.9, ...), custom_call_target="tpu_custom_call" | custom-call | tf_op jit(solution)/shard_map/layer/pallas_call | solution.py:291
  51.8 0.7 %copy.15 = bf16[256,256]{1,0:T(8,128)(2,1)} copy(bf16[256,256]{1,0:T(8,128)(2,1)S(1)} %get-tuple-element.6) | data formatting | bytes 262144
  52.4 0.7 %copy.16 = f32[256,256]{1,0:T(8,128)} copy(f32[256,256]{1,0:T(8,128)S(1)} %get-tuple-element.7) | data formatting | bytes 524288
  53.1 0.7 %copy.17 = bf16[256,256]{1,0:T(8,128)(2,1)} copy(bf16[256,256]{1,0:T(8,128)(2,1)S(1)} %get-tuple-element.8) | data formatting | bytes 262144
Async XLA Ops:
  0.6 6.9 %copy-start.6 = (s32[256]{0:T(256)S(1)}, s32[256]{0:T(256)}, u32[]{:S(2)}) copy-start(s32[256]{0:T(256)} %param.10) | copy-start | bytes 3076
  1.3 1.6 %copy-start = (s32[1,1,256,16,128]{4,3,2,1,0:T(8,128)S(1)}, s32[1,1,256,16,128]{4,3,2,1,0:T(8,128)}, u32[]{:S(2)}) copy-start(s32[1,1,256,16,128]{4,3,2,1,0:T(8,128)} %param.14) | copy-start | bytes 6291460
  2.9 0.7 %copy-start.4 = (s32[1,1,256]{2,1,0:T(1,128)S(1)}, s32[1,1,256]{2,1,0:T(1,128)}, u32[]{:S(2)}) copy-start(s32[1,1,256]{2,1,0:T(1,128)} %param.12) | copy-start | bytes 3076
  3.6 0.7 %copy-start.5 = (s32[1,1,256]{2,1,0:T(1,128)S(1)}, s32[1,1,256]{2,1,0:T(1,128)}, u32[]{:S(2)}) copy-start(s32[1,1,256]{2,1,0:T(1,128)} %param.13) | copy-start | bytes 3076
  4.3 3.3 %copy-start.1 = (bf16[256,256]{1,0:T(8,128)(2,1)S(1)}, bf16[256,256]{1,0:T(8,128)(2,1)}, u32[]{:S(2)}) copy-start(bf16[256,256]{1,0:T(8,128)(2,1)} %feat_ref.1) | copy-start | bytes 393220
  4.3 3.3 %copy-start.2 = (bf16[256,256]{1,0:T(8,128)(2,1)S(1)}, bf16[256,256]{1,0:T(8,128)(2,1)}, u32[]{:S(2)}) copy-start(bf16[256,256]{1,0:T(8,128)(2,1)} %cot_ref.1) | copy-start | bytes 393220
  4.3 3.3 %copy-start.3 = (bf16[256,256]{1,0:T(8,128)(2,1)S(1)}, bf16[256,256]{1,0:T(8,128)(2,1)}, u32[]{:S(2)}) copy-start(bf16[256,256]{1,0:T(8,128)(2,1)} %weight_ref.1) | copy-start | bytes 393220

commit v3 on v2

--- a/solution.py
+++ b/solution.py
@@ -92,31 +92,45 @@
 
 def layer_kernel(
     n_row, n_z,
-    at_ref, feat_ref, cot_ref, deg_ref, weight_ref,
+    rows_ref, cols_ref, count_ref, deg_ref, bits_hbm, feat_hbm, cot_hbm, weight_hbm,
     out_ref, wgrad_ref, igrad_ref,
-    feats, grads, part, pair, sums, arrived, back, back_in, w_part, w_in, w_all,
+    at_ref, prefix, plan, plan_smem, bits_ref, feat_ref, cot_ref, weight_ref, load_s, plan_s,
+    feats, grads, part, pair, sums, arrived, back, back_in, w_part, w_in, w_mid, w_all,
     feat_s, feat_r, grad_s, grad_r, relay_s, pair_s, pair_r, sum_s, sum_r, back_s, back_r,
-    w1_s, w1_r, w2_s, w2_r,
+    w1_s, w1_r, w2_s, w2_r, w3_s, w3_r,
 ):
     n = feat_ref.shape[0]
     n_col = 2 * n_z
-    n_all = n_row * n_col
+    n_plane = n_row * 2
     r = lax.axis_index("row")
     c = lax.axis_index("col")
-    me = r * n_col + c
     z = c // 2
     core = c % 2
     sibling = (r, z * 2 + 1 - core)
 
-    def peer_of(i):
-        peer = (me + i) % n_all
-        return peer, (peer // n_col, peer % n_col)
+    me = r * 2 + core
+
+    def plane_peer(i):
+        q = (me + i) % n_plane
+        return q, (q // 2, z * 2 + q % 2)
+
+    def z_peer(i):
+        zz = (z + i) % n_z
+        return zz, (r, zz * 2 + core)
 
     barrier = pltpu.get_barrier_semaphore()
-
-    @pl.loop(1, n_all)
-    def _(i):
-        pl.semaphore_signal(barrier, inc=1, device_id=peer_of(i)[1], device_id_type=MESH)
+    for i in range(1, n_plane):
+        pl.semaphore_signal(barrier, inc=1, device_id=plane_peer(i)[1], device_id_type=MESH)
+    for i in range(1, n_z):
+        pl.semaphore_signal(barrier, inc=1, device_id=z_peer(i)[1], device_id_type=MESH)
+    loads = [
+        pltpu.make_async_copy(src, dst, load_s.at[k])
+        for k, (src, dst) in enumerate(
+            ((cot_hbm, cot_ref), (feat_hbm, feat_ref), (bits_hbm, bits_ref), (weight_hbm, weight_ref))
+        )
+    ]
+    for load in loads:
+        load.start()
 
     i0 = lax.broadcasted_iota(jnp.int32, (n, n), 0)
     i1 = lax.broadcasted_iota(jnp.int32, (n, n), 1)
@@ -124,10 +138,31 @@
     order = (i0 == placed).astype(F32).astype(BF16)
     deg_row = deg_ref[...].astype(F32)
     deg_col = jnp.sum(jnp.where(i0 == i1, deg_row, 0.0), axis=1, keepdims=True)
+
+    trows = n * n_col // 128
+    tcols = n * n_row // 128
+    places = trows * tcols
+    slots = rows_ref.shape[1]
+    s0 = lax.broadcasted_iota(jnp.int32, (slots, slots), 0)
+    s1 = lax.broadcasted_iota(jnp.int32, (slots, slots), 1)
+    lane = lax.broadcasted_iota(jnp.int32, (1, slots), 1)
+    place = jnp.where(lane < count_ref[...], cols_ref[...] * trows + rows_ref[...], places)
+    key_row = (place * slots + lane).astype(F32)
+    key_col = jnp.sum(jnp.where(s0 == s1, key_row, 0.0), axis=1, keepdims=True)
+    rank = jnp.sum((key_row < key_col).astype(F32), axis=1, keepdims=True)
+    picked = jnp.where(rank == s1.astype(F32), s0, 0)
+    before = (key_col < (s1 * slots).astype(F32)).astype(jnp.int32)
+    plan[0:1, :] = jnp.clip(jnp.sum(picked, axis=0, keepdims=True), 0, slots - 1)
+    plan[1:2, :] = jnp.clip(jnp.sum(before, axis=0, keepdims=True), 0, slots)
+    plan_copy = pltpu.make_async_copy(plan, plan_smem, plan_s)
+    plan_copy.start()
+
+    loads[0].wait()
+    loads[1].wait()
     grads[c] = (cot_ref[...].astype(F32) / deg_col).astype(BF16)
     feats[r] = dot(feat_ref[...], order, ((0,), (0,))).astype(BF16)
 
-    pl.semaphore_wait(barrier, n_all - 1)
+    pl.semaphore_wait(barrier, n_plane + n_z - 2)
 
     def feat_copy(i):
         q = (r + i) % n_row
@@ -148,6 +183,36 @@
 
     def arrive(ref, sem, slot):
         copy_to(ref.at[slot], ref.at[slot], sem.at[slot], sem.at[slot], sibling).wait_recv()
+
+    plan_copy.wait()
+    loads[2].wait()
+    zero = jnp.zeros((8, 128), jnp.int32)
+    for b in range(8):
+        prefix[0, b] = zero
+
+    def add_slot(k, totals):
+        words = bits_ref[plan_smem[0, k]]
+        word = words[:8] | (words[8:] << 16)
+        totals = tuple(t + ((word >> b) & 0x10001) for b, t in enumerate(totals))
+        for b in range(8):
+            prefix[k + 1, b] = totals[b]
+        return totals
+
+    lax.fori_loop(0, slots, add_slot, (zero,) * 8, unroll=4)
+
+    def place_row(row, carry):
+        lanes = pl.ds(pl.multiple_of(row * 128, 128), 128)
+        for col in range(tcols):
+            p = col * trows + row
+            first = plan_smem[1, p]
+            last = plan_smem[1, p + 1]
+            for b in range(8):
+                v = prefix[last, b] - prefix[first, b]
+                both = jnp.concatenate([v & 0xFFFF, v >> 16], axis=0)
+                at_ref[pl.ds(col * 128 + b * 16, 16), lanes] = both.astype(F32).astype(BF16)
+        return carry
+
+    lax.fori_loop(0, trows, place_row, 0)
 
     for i in range(1, n_row):
         arrive(feats, feat_r, (r + i) % n_row)
@@ -209,45 +274,34 @@
     local = dot(part[0], grads[0])
     for q in range(1, n_col):
         local += dot(part[q], grads[q])
-    blocks = [(pl.ds((d // 2) * 16, 16), pl.ds((d % 2) * 128, 128)) for d in range(n_all)]
     rounded = local.astype(BF16)
-    for d in range(n_all):
-        top, left = (d // 2) * 16, (d % 2) * 128
-        w_part[d] = rounded[top : top + 16, left : left + 128]
+    slab = rounded.shape[0] // n_plane
+    for d in range(n_plane):
+        w_part[d] = rounded[d * slab : (d + 1) * slab]
 
     def w1_copy(i):
-        peer, device = peer_of(i)
-        return copy_to(w_part.at[peer], w_in.at[me], w1_s.at[peer], w1_r.at[me], device)
+        q, device = plane_peer(i)
+        return copy_to(w_part.at[q], w_in.at[me], w1_s.at[q], w1_r.at[me], device)
 
     def w2_copy(i):
-        peer, device = peer_of(i)
-        return copy_to(w_all.at[me], w_all.at[me], w2_s.at[peer], w2_r.at[me], device)
-
-    @pl.loop(1, n_all)
-    def _(i):
+        q, device = z_peer(i)
+        return copy_to(w_mid.at[z], w_mid.at[z], w2_s.at[q], w2_r.at[z], device)
+
+    def w3_copy(i):
+        q, device = plane_peer(i)
+        return copy_to(w_all.at[me], w_all.at[me], w3_s.at[q], w3_r.at[me], device)
+
+    for i in range(1, n_plane):
         w1_copy(i).start()
-
     backward(r)
     w_in[me] = w_part[me]
-
-    @pl.loop(1, n_all)
-    def _(i):
-        arrive(w_in, w1_r, (me + i) % n_all)
-
-    w_all[me] = jnp.sum(w_in[...].astype(F32), axis=0).astype(BF16)
-
-    @pl.loop(1, n_all)
-    def _(i):
+    for i in range(1, n_plane):
+        arrive(w_in, w1_r, (me + i) % n_plane)
+    w_mid[z] = jnp.sum(w_in[...].astype(F32), axis=0).astype(BF16)
+    for i in range(1, n_z):
         w2_copy(i).start()
 
-    arrive(pair, pair_r, z)
-    total = part[c].astype(F32) + pair[z].astype(F32)
-    for i in range(1, n_z):
-        zz = (z + i) % n_z
-        arrive(arrived, sum_r, zz)
-        total += arrived[zz].astype(F32)
-    out_ref[...] = dot((total / deg_row).astype(BF16), weight_ref[...], ((0,), (0,))).astype(BF16)
-
+    loads[3].wait()
     total = back[r].astype(F32)
     for i in range(1, n_row):
         q = (r + i) % n_row
@@ -256,12 +310,24 @@
     ordered = dot(order, total.astype(BF16)).astype(BF16)
     igrad_ref[...] = dot(ordered, weight_ref[...], ((1,), (1,))).astype(BF16)
 
-    @pl.loop(1, n_all)
-    def _(i):
-        arrive(w_all, w2_r, (me + i) % n_all)
-
-    for d in range(n_all):
-        wgrad_ref[blocks[d]] = w_all[d].astype(F32)
+    for i in range(1, n_z):
+        arrive(w_mid, w2_r, (z + i) % n_z)
+    w_all[me] = jnp.sum(w_mid[...].astype(F32), axis=0).astype(BF16)
+    for i in range(1, n_plane):
+        w3_copy(i).start()
+
+    arrive(pair, pair_r, z)
+    total = part[c].astype(F32) + pair[z].astype(F32)
+    for i in range(1, n_z):
+        zz = (z + i) % n_z
+        arrive(arrived, sum_r, zz)
+        total += arrived[zz].astype(F32)
+    out_ref[...] = dot((total / deg_row).astype(BF16), weight_ref[...], ((0,), (0,))).astype(BF16)
+
+    for i in range(1, n_plane):
+        arrive(w_all, w3_r, (me + i) % n_plane)
+    for d in range(n_plane):
+        wgrad_ref[d * slab : (d + 1) * slab, :] = w_all[d].astype(F32)
 
     for i in range(1, n_row):
         feat_copy(i)[1].wait_send()
@@ -274,37 +340,48 @@
         relay_copy(zz * 2 + core).wait_send()
         pair_copy(zz).wait_send()
 
-    @pl.loop(1, n_all)
-    def _(i):
+    for i in range(1, n_plane):
         w1_copy(i).wait_send()
+        w3_copy(i).wait_send()
+    for i in range(1, n_z):
         w2_copy(i).wait_send()
 
 
-def layer(at, features, cotangent, degrees, weight, n_row, n_z):
+def layer(rows, cols, count, bits, features, cotangent, degrees, weight, n_row, n_z):
     n, width = features.shape
     n_col = 2 * n_z
-    n_all = n_row * n_col
+    n_plane = 2 * n_row
+    slots = bits.shape[0]
     block = lambda k: pltpu.VMEM((k, n, width), BF16)
     sems = lambda k: pltpu.SemaphoreType.DMA((k,))
-    small = pltpu.VMEM((n_all, 16, 128), BF16)
+    slab = lambda k: pltpu.VMEM((k, width // n_plane, width), BF16)
     tile = jax.ShapeDtypeStruct((n, width), BF16)
     return pl.pallas_call(
         functools.partial(layer_kernel, n_row, n_z),
         out_shape=(tile, jax.ShapeDtypeStruct((width, width), F32), tile),
-        in_specs=[pl.BlockSpec(memory_space=VMEM)] * 5,
+        in_specs=[pl.BlockSpec(memory_space=VMEM)] * 4 + [pl.BlockSpec(memory_space=pl.ANY)] * 4,
         out_specs=(pl.BlockSpec(memory_space=VMEM),) * 3,
         scratch_shapes=[
+            pltpu.VMEM((n * n_row, n * n_col), BF16),
+            pltpu.VMEM((slots + 1, 8, 8, 128), jnp.int32),
+            pltpu.VMEM((2, slots), jnp.int32),
+            pltpu.SMEM((2, slots), jnp.int32),
+            pltpu.VMEM(bits.shape, jnp.int32),
+            pltpu.VMEM((n, width), BF16),
+            pltpu.VMEM((n, width), BF16),
+            pltpu.VMEM((width, width), BF16),
+            sems(4), pltpu.SemaphoreType.DMA,
             block(n_row), block(n_col), block(n_col), block(n_z), block(n_z), block(n_z),
-            block(n_row), block(n_row), small, small, small,
+            block(n_row), block(n_row), slab(n_plane), slab(n_plane), slab(n_z), slab(n_plane),
             sems(n_row), sems(n_row), sems(n_col), sems(n_col), sems(n_z), sems(n_z), sems(n_z),
             sems(n_z), sems(n_z), sems(n_row), sems(n_row),
-            sems(n_all), sems(n_all), sems(n_all), sems(n_all),
+            sems(n_plane), sems(n_plane), sems(n_z), sems(n_z), sems(n_plane), sems(n_plane),
         ],
         compiler_params=pltpu.CompilerParams(
             collective_id=0, has_side_effects=True, vmem_limit_bytes=48 * 2**20
         ),
         name="layer",
-    )(at, features, cotangent, degrees, weight)
+    )(rows, cols, count, degrees, bits, features, cotangent, weight)
 
 
 def swap_order(x, a, b):
@@ -315,14 +392,16 @@
     nodes, width = features.shape
     trows = nodes * lax.axis_size("col") // 128
     tcols = nodes * lax.axis_size("row") // 128
+    n_row, n_col = lax.axis_size("row"), lax.axis_size("col")
+    slots = tile_bits.shape[2]
+    if n_row * n_col == 32 and nodes == width and trows * tcols < slots:
+        return layer(
+            tile_rows[0], tile_cols[0], tile_count, tile_bits[0, 0],
+            features, cotangent, degrees.reshape(1, nodes), weight, n_row, n_col // 2,
+        )
     at = build_adjacency(
         tile_count[0], tile_rows[0, 0], tile_cols[0, 0], tile_bits[0, 0], trows, tcols
     )
-    n_row, n_col = lax.axis_size("row"), lax.axis_size("col")
-    if n_row * n_col * 16 * 128 == width * width and nodes == width:
-        return layer(
-            at, features, cotangent, degrees.reshape(1, nodes), weight, n_row, n_col // 2
-        )
     deg = degrees[:, None].astype(F32)
     scaled = (cotangent.astype(F32) / deg).astype(BF16)
     feats = lax.all_gather(swap_order(features, 16, 8), "row", axis=0, tiled=True)

time: 53.8 us -> 51.5 us (0.957)
  Pallas kernels: 47.4 us -> 41.6 us
  local copies, waits for them, and re-layouts: 4.97 us -> 8.35 us
    unnamed x17, local copies, waits for them, and re-layouts: 4.97 us -> 8.35 us
    pallas_call x1 -> x0, Pallas kernels: 3.27 us -> none  [build_adjacency(): pl.pallas_call(functools.partial(build_kernel, trows, chunk), grid=(tcols...]
    pallas_call x1, Pallas kernels: 44.2 us -> 41.6 us  [layer(): pl.pallas_call(functools.partial(layer_kernel, n_row, n_z), out_shape=(ti...]
where the time goes in v3:
time: 51.5 us; the launch traced here: 51.3 us
  Pallas kernels  41.6 us (81%)
  local copies, waits for them, and re-layouts  8.35 us (16%)
  between operations  1.3 us (3%)
    pallas_call x1, Pallas kernels, layer(): pl.pallas_call(functools.partial(layer_kernel, n_row, n_z), out_shape=(ti...  41.6 us
    unnamed x17, local copies, waits for them, and re-layouts  8.35 us

profile of v3, /device:TPU:0, one launch (start us, length us, event | category | flops | bytes accessed | tf_op | source)
XLA Modules:
  0.0 51.3 jit_solution(14046756585648782731)
XLA Ops:
  1.3 0.0 copy-start
  1.3 1.6 %copy-done = s32[1,1,256,16,128]{4,3,2,1,0:T(8,128)S(1)} copy-done((s32[1,1,256,16,128]{4,3,2,1,0:T(8,128)S(1)}, s32[1,1,256,16,128]{4,3,2,1,0:T(8,128)}, u32[]{:S(2)}) %copy-start) | copy-done | bytes 2097176
  2.9 0.0 copy-start.1
  2.9 0.9 %copy-done.1 = bf16[256,256]{1,0:T(8,128)(2,1)S(1)} copy-done((bf16[256,256]{1,0:T(8,128)(2,1)S(1)}, bf16[256,256]{1,0:T(8,128)(2,1)}, u32[]{:S(2)}) %copy-start.1) | copy-done | bytes 131096
  3.8 0.0 copy-start.2
  3.8 0.9 %copy-done.2 = bf16[256,256]{1,0:T(8,128)(2,1)S(1)} copy-done((bf16[256,256]{1,0:T(8,128)(2,1)S(1)}, bf16[256,256]{1,0:T(8,128)(2,1)}, u32[]{:S(2)}) %copy-start.2) | copy-done | bytes 131096
  4.7 0.0 copy-start.3
  4.7 0.9 %copy-done.3 = bf16[256,256]{1,0:T(8,128)(2,1)S(1)} copy-done((bf16[256,256]{1,0:T(8,128)(2,1)S(1)}, bf16[256,256]{1,0:T(8,128)(2,1)}, u32[]{:S(2)}) %copy-start.3) | copy-done | bytes 131096
  5.6 0.0 copy-start.4
  5.6 0.7 %copy-done.4 = s32[1,1,256]{2,1,0:T(1,128)S(1)} copy-done((s32[1,1,256]{2,1,0:T(1,128)S(1)}, s32[1,1,256]{2,1,0:T(1,128)}, u32[]{:S(2)}) %copy-start.4) | copy-done | bytes 1048
  6.3 0.0 copy-start.5
  6.3 0.7 %copy-done.5 = s32[1,1,256]{2,1,0:T(1,128)S(1)} copy-done((s32[1,1,256]{2,1,0:T(1,128)S(1)}, s32[1,1,256]{2,1,0:T(1,128)}, u32[]{:S(2)}) %copy-start.5) | copy-done | bytes 1048
  6.9 0.0 copy-start.6
  6.9 0.7 %copy-done.6 = s32[256]{0:T(256)S(1)} copy-done((s32[256]{0:T(256)S(1)}, s32[256]{0:T(256)}, u32[]{:S(2)}) %copy-start.6) | copy-done | bytes 1048
  7.6 41.6 %layer.1 = (bf16[256,256]{1,0:T(8,128)(2,1)S(1)}, f32[256,256]{1,0:T(8,128)S(1)}, bf16[256,256]{1,0:T(8,128)(2,1)S(1)}) custom-call(s32[1,256]{1,0:T(1,128)S(1)} %bitcast.5, s32[1,256]{1,0:T(1,128)S(1)} %bitcast.6, s32[1,1]{1,0:T(1,128)S(6)} %copy.14.count_ref, s32[1,256]{1,0:T(1,128)S(1)} %bitcast.7, s32[256,16,128]{2,1,0:T(8,128)S(1)} %bitcast.4, ...), custom_call_target="tpu_custom_call" | custom-call | tf_op jit(solution)/shard_map/layer/pallas_call | solution.py:359
  49.2 0.7 %copy.15 = bf16[256,256]{1,0:T(8,128)(2,1)} copy(bf16[256,256]{1,0:T(8,128)(2,1)S(1)} %get-tuple-element.6) | data formatting | bytes 262144
  49.9 0.7 %copy.16 = f32[256,256]{1,0:T(8,128)} copy(f32[256,256]{1,0:T(8,128)S(1)} %get-tuple-element.7) | data formatting | bytes 524288
  50.6 0.7 %copy.17 = bf16[256,256]{1,0:T(8,128)(2,1)} copy(bf16[256,256]{1,0:T(8,128)(2,1)S(1)} %get-tuple-element.8) | data formatting | bytes 262144
Async XLA Ops:
  1.3 1.6 %copy-start = (s32[1,1,256,16,128]{4,3,2,1,0:T(8,128)S(1)}, s32[1,1,256,16,128]{4,3,2,1,0:T(8,128)}, u32[]{:S(2)}) copy-start(s32[1,1,256,16,128]{4,3,2,1,0:T(8,128)} %param.14) | copy-start | bytes 6291460
  2.9 0.9 %copy-start.1 = (bf16[256,256]{1,0:T(8,128)(2,1)S(1)}, bf16[256,256]{1,0:T(8,128)(2,1)}, u32[]{:S(2)}) copy-start(bf16[256,256]{1,0:T(8,128)(2,1)} %feat_hbm.1) | copy-start | bytes 393220
  3.8 0.9 %copy-start.2 = (bf16[256,256]{1,0:T(8,128)(2,1)S(1)}, bf16[256,256]{1,0:T(8,128)(2,1)}, u32[]{:S(2)}) copy-start(bf16[256,256]{1,0:T(8,128)(2,1)} %cot_hbm.1) | copy-start | bytes 393220
  4.7 0.9 %copy-start.3 = (bf16[256,256]{1,0:T(8,128)(2,1)S(1)}, bf16[256,256]{1,0:T(8,128)(2,1)}, u32[]{:S(2)}) copy-start(bf16[256,256]{1,0:T(8,128)(2,1)} %weight_hbm.1) | copy-start | bytes 393220
  5.6 0.7 %copy-start.4 = (s32[1,1,256]{2,1,0:T(1,128)S(1)}, s32[1,1,256]{2,1,0:T(1,128)}, u32[]{:S(2)}) copy-start(s32[1,1,256]{2,1,0:T(1,128)} %param.12) | copy-start | bytes 3076
  6.3 0.7 %copy-start.5 = (s32[1,1,256]{2,1,0:T(1,128)S(1)}, s32[1,1,256]{2,1,0:T(1,128)}, u32[]{:S(2)}) copy-start(s32[1,1,256]{2,1,0:T(1,128)} %param.13) | copy-start | bytes 3076
  6.9 0.7 %copy-start.6 = (s32[256]{0:T(256)S(1)}, s32[256]{0:T(256)}, u32[]{:S(2)}) copy-start(s32[256]{0:T(256)} %param.10) | copy-start | bytes 3076

commit v4 on v3

--- a/solution.py
+++ b/solution.py
@@ -95,8 +95,8 @@
     rows_ref, cols_ref, count_ref, deg_ref, bits_hbm, feat_hbm, cot_hbm, weight_hbm,
     out_ref, wgrad_ref, igrad_ref,
     at_ref, prefix, plan, plan_smem, bits_ref, feat_ref, cot_ref, weight_ref, load_s, plan_s,
-    feats, grads, part, pair, sums, arrived, back, back_in, w_part, w_in, w_mid, w_all,
-    feat_s, feat_r, grad_s, grad_r, relay_s, pair_s, pair_r, sum_s, sum_r, back_s, back_r,
+    feats, grads, part, pair, sums, passed, arrived, back, back_in, w_part, w_in, w_mid, w_all,
+    feat_s, feat_r, grad_s, grad_r, relay_s, on_s, pair_s, pair_r, sum_s, sum_r, pass_r, back_s, back_r,
     w1_s, w1_r, w2_s, w2_r, w3_s, w3_r,
 ):
     n = feat_ref.shape[0]
@@ -117,6 +117,16 @@
     def z_peer(i):
         zz = (z + i) % n_z
         return zz, (r, zz * 2 + core)
+
+    def flip(i):
+        return ((z // 2 + i // 2) % 2) * 2 + (z + i) % 2
+
+    mate = flip(1)
+    inner = z % 2 != z // 2
+    end = z % 2 == z // 2
+
+    def at_z(zz):
+        return (r, zz * 2 + core)
 
     barrier = pltpu.get_barrier_semaphore()
     for i in range(1, n_plane):
@@ -168,17 +178,21 @@
         q = (r + i) % n_row
         return q, copy_to(feats.at[r], feats.at[r], feat_s.at[q], feat_r.at[r], (q, c))
 
-    def grad_copy(i):
-        q = ((z + i) % n_z) * 2 + core
-        return q, copy_to(grads.at[c], grads.at[c], grad_s.at[q], grad_r.at[c], (r, q))
+    def grad_copy(k):
+        zz = (2 - z // 2, mate)[k]
+        return copy_to(grads.at[c], grads.at[c], grad_s.at[k], grad_r.at[c], at_z(zz))
+
+    def on_copy(i):
+        q = flip(i) * 2 + core
+        return copy_to(grads.at[q], grads.at[q], on_s.at[i], grad_r.at[q], at_z(mate))
 
     def relay_copy(q):
         return copy_to(grads.at[q], grads.at[q], relay_s.at[q // 2], grad_r.at[q], sibling)
 
     for i in range(1, n_row):
         feat_copy(i)[1].start()
-    for i in range(1, n_z):
-        grad_copy(i)[1].start()
+    for k in range(2):
+        grad_copy(k).start()
     relay_copy(c).start()
 
     def arrive(ref, sem, slot):
@@ -214,6 +228,14 @@
 
     lax.fori_loop(0, trows, place_row, 0)
 
+    @pl.when(inner)
+    def _():
+        for i in (3, 2):
+            q = flip(i) * 2 + core
+            arrive(grads, grad_r, q)
+            on_copy(i).start()
+            relay_copy(q).start()
+
     for i in range(1, n_row):
         arrive(feats, feat_r, (r + i) % n_row)
 
@@ -228,35 +250,50 @@
         q = zz * 2 + 1 - core
         return copy_to(part.at[q], pair.at[zz], pair_s.at[zz], pair_r.at[zz], sibling)
 
-    @pl.loop(1, n_z + 1)
+    @pl.loop(0, n_z)
     def _(i):
-        zz = (z + i) % n_z
+        zz = flip(3 - i)
         forward(zz * 2 + 1 - core)
         pair_copy(zz).start()
 
-    @pl.loop(1, n_z + 1)
+    @pl.loop(0, n_z)
     def _(i):
-        forward(((z + i) % n_z) * 2 + core)
+        forward(flip(3 - i) * 2 + core)
+
+    def paired(zz):
+        arrive(pair, pair_r, zz)
+        return part[zz * 2 + core].astype(F32) + pair[zz].astype(F32)
+
+    def pass_copy(i):
+        zz = flip(i)
+        return copy_to(sums.at[zz], passed.at[zz], sum_s.at[zz], pass_r.at[zz], at_z(mate))
 
     def sum_copy(i):
-        zz = (z + i) % n_z
-        return copy_to(
-            sums.at[zz], arrived.at[z], sum_s.at[zz], sum_r.at[z], (r, zz * 2 + core)
-        )
-
-    @pl.loop(1, n_z)
-    def _(i):
-        zz = (z + i) % n_z
-        arrive(pair, pair_r, zz)
-        sums[zz] = (part[zz * 2 + core].astype(F32) + pair[zz].astype(F32)).astype(BF16)
-        sum_copy(i).start()
-
-    for i in range(1, n_z):
-        q = ((z + i) % n_z) * 2 + core
-        arrive(grads, grad_r, q)
-        relay_copy(q).start()
+        zz = flip(i)
+        k = 0 if i == 1 else 1
+        return copy_to(sums.at[zz], arrived.at[k], sum_s.at[zz], sum_r.at[k], at_z(zz))
+
+    @pl.when(end)
+    def _():
+        for i in (3, 2):
+            sums[flip(i)] = paired(flip(i)).astype(BF16)
+            pass_copy(i).start()
+
+    sums[mate] = paired(mate).astype(BF16)
+    sum_copy(1).start()
+
+    arrive(grads, grad_r, mate * 2 + core)
+    relay_copy(mate * 2 + core).start()
+
+    @pl.when(end)
+    def _():
+        for i in (2, 3):
+            q = flip(i) * 2 + core
+            arrive(grads, grad_r, q)
+            relay_copy(q).start()
+
     for i in range(n_z):
-        arrive(grads, grad_r, ((z + i) % n_z) * 2 + 1 - core)
+        arrive(grads, grad_r, flip(i) * 2 + 1 - core)
 
     def back_copy(q):
         return copy_to(back.at[q], back_in.at[r], back_s.at[q], back_r.at[r], (q, c))
@@ -270,6 +307,15 @@
         q = (r + i) % n_row
         backward(q)
         back_copy(q).start()
+
+    @pl.when(inner)
+    def _():
+        for i in (2, 3):
+            zz = flip(i)
+            total = paired(zz)
+            arrive(passed, pass_r, zz)
+            sums[zz] = (total + passed[zz].astype(F32)).astype(BF16)
+            sum_copy(i).start()
 
     local = dot(part[0], grads[0])
     for q in range(1, n_col):
@@ -316,12 +362,10 @@
     for i in range(1, n_plane):
         w3_copy(i).start()
 
-    arrive(pair, pair_r, z)
-    total = part[c].astype(F32) + pair[z].astype(F32)
-    for i in range(1, n_z):
-        zz = (z + i) % n_z
-        arrive(arrived, sum_r, zz)
-        total += arrived[zz].astype(F32)
+    total = paired(z)
+    for k in range(2):
+        arrive(arrived, sum_r, k)
+        total += arrived[k].astype(F32)
     out_ref[...] = dot((total / deg_row).astype(BF16), weight_ref[...], ((0,), (0,))).astype(BF16)
 
     for i in range(1, n_plane):
@@ -332,9 +376,21 @@
     for i in range(1, n_row):
         feat_copy(i)[1].wait_send()
         back_copy((r + i) % n_row).wait_send()
-    for i in range(1, n_z):
-        grad_copy(i)[1].wait_send()
-        sum_copy(i).wait_send()
+    for k in range(2):
+        grad_copy(k).wait_send()
+    sum_copy(1).wait_send()
+
+    @pl.when(inner)
+    def _():
+        for i in (2, 3):
+            on_copy(i).wait_send()
+            sum_copy(i).wait_send()
+
+    @pl.when(end)
+    def _():
+        for i in (2, 3):
+            pass_copy(i).wait_send()
+
     for i in range(n_z):
         zz = (z + i) % n_z
         relay_copy(zz * 2 + core).wait_send()
@@ -371,14 +427,14 @@
             pltpu.VMEM((n, width), BF16),
             pltpu.VMEM((width, width), BF16),
             sems(4), pltpu.SemaphoreType.DMA,
-            block(n_row), block(n_col), block(n_col), block(n_z), block(n_z), block(n_z),
+            block(n_row), block(n_col), block(n_col), block(n_z), block(n_z), block(n_z), block(2),
             block(n_row), block(n_row), slab(n_plane), slab(n_plane), slab(n_z), slab(n_plane),
-            sems(n_row), sems(n_row), sems(n_col), sems(n_col), sems(n_z), sems(n_z), sems(n_z),
-            sems(n_z), sems(n_z), sems(n_row), sems(n_row),
+            sems(n_row), sems(n_row), sems(2), sems(n_col), sems(n_z), sems(4), sems(n_z), sems(n_z),
+            sems(n_z), sems(2), sems(n_z), sems(n_row), sems(n_row),
             sems(n_plane), sems(n_plane), sems(n_z), sems(n_z), sems(n_plane), sems(n_plane),
         ],
         compiler_params=pltpu.CompilerParams(
-            collective_id=0, has_side_effects=True, vmem_limit_bytes=48 * 2**20
+            collective_id=0, has_side_effects=True, vmem_limit_bytes=64 * 2**20
         ),
         name="layer",
     )(rows, cols, count, degrees, bits, features, cotangent, weight)
@@ -394,7 +450,7 @@
     tcols = nodes * lax.axis_size("row") // 128
     n_row, n_col = lax.axis_size("row"), lax.axis_size("col")
     slots = tile_bits.shape[2]
-    if n_row * n_col == 32 and nodes == width and trows * tcols < slots:
+    if n_row == 4 and n_col == 8 and nodes == width and trows * tcols < slots:
         return layer(
             tile_rows[0], tile_cols[0], tile_count, tile_bits[0, 0],
             features, cotangent, degrees.reshape(1, nodes), weight, n_row, n_col // 2,

time: 51.5 us -> 46.4 us (0.901)
  local copies, waits for them, and re-layouts: 8.35 us -> 4.8 us
  Pallas kernels: 41.6 us -> 40 us
    unnamed x17 -> x3, local copies, waits for them, and re-layouts: 8.35 us -> 4.8 us
    pallas_call x1, Pallas kernels: 41.6 us -> 40 us  [layer(): pl.pallas_call(functools.partial(layer_kernel, n_row, n_z), out_shape=(ti...]
where the time goes in v4:
time: 46.4 us; the launch traced here: 46.1 us
  Pallas kernels  40 us (86%)
  local copies, waits for them, and re-layouts  4.8 us (10%)
  between operations  1.29 us (3%)
    pallas_call x1, Pallas kernels, layer(): pl.pallas_call(functools.partial(layer_kernel, n_row, n_z), out_shape=(ti...  40 us
    unnamed x3, local copies, waits for them, and re-layouts  4.8 us

profile of v4, /device:TPU:0, one launch (start us, length us, event | category | flops | bytes accessed | tf_op | source)
XLA Modules:
  0.0 46.1 jit_solution(13655557553676281262)
XLA Ops:
  1.3 40.0 %layer.1 = (bf16[256,256]{1,0:T(8,128)(2,1)}, f32[256,256]{1,0:T(8,128)}, bf16[256,256]{1,0:T(8,128)(2,1)}) custom-call(s32[1,256]{1,0:T(1,128)} %bitcast.5, s32[1,256]{1,0:T(1,128)} %bitcast.6, s32[1,1]{1,0:T(1,128)S(6)} %copy.14.count_ref, s32[1,256]{1,0:T(1,128)} %bitcast.7, s32[256,16,128]{2,1,0:T(8,128)} %bitcast.4, bf16[256,256]{1,0:T(8,128)(2,1)} %feat_hbm.1, ...), custom_call_target="tpu_custom_call" | custom-call | tf_op jit(solution)/shard_map/layer/pallas_call | solution.py:415
  41.3 1.6 %copy.15 = bf16[256,256]{1,0:T(8,128)(2,1)} copy(bf16[256,256]{1,0:T(8,128)(2,1)} %get-tuple-element.6) | data formatting | bytes 262144
  42.9 1.7 %copy.16 = f32[256,256]{1,0:T(8,128)} copy(f32[256,256]{1,0:T(8,128)} %get-tuple-element.7) | data formatting | bytes 524288
  44.6 1.6 %copy.17 = bf16[256,256]{1,0:T(8,128)(2,1)} copy(bf16[256,256]{1,0:T(8,128)(2,1)} %get-tuple-element.8) | data formatting | bytes 262144

commit v5 on v4

--- a/solution.py
+++ b/solution.py
@@ -92,11 +92,11 @@
 
 def layer_kernel(
     n_row, n_z,
-    rows_ref, cols_ref, count_ref, deg_ref, bits_hbm, feat_hbm, cot_hbm, weight_hbm,
+    count_ref, rows_hbm, cols_hbm, deg_hbm, bits_hbm, feat_hbm, cot_hbm, weight_hbm,
     out_ref, wgrad_ref, igrad_ref,
-    at_ref, prefix, plan, plan_smem, bits_ref, feat_ref, cot_ref, weight_ref, load_s, plan_s,
+    at_ref, prefix, plan, plan_smem, rows_ref, cols_ref, deg_ref, bits_ref, feat_ref, cot_ref, weight_ref, load_s, plan_s,
     feats, grads, part, pair, sums, passed, arrived, back, back_in, w_part, w_in, w_mid, w_all,
-    feat_s, feat_r, grad_s, grad_r, relay_s, on_s, pair_s, pair_r, sum_s, sum_r, pass_r, back_s, back_r,
+    feat_s, feat_r, grad_s, grad_r, relay_s, pair_s, pair_r, sum_s, sum_r, pass_r, back_s, back_r,
     w1_s, w1_r, w2_s, w2_r, w3_s, w3_r,
 ):
     n = feat_ref.shape[0]
@@ -136,7 +136,10 @@
     loads = [
         pltpu.make_async_copy(src, dst, load_s.at[k])
         for k, (src, dst) in enumerate(
-            ((cot_hbm, cot_ref), (feat_hbm, feat_ref), (bits_hbm, bits_ref), (weight_hbm, weight_ref))
+            (
+                (rows_hbm, rows_ref), (cols_hbm, cols_ref), (deg_hbm, deg_ref), (cot_hbm, cot_ref),
+                (feat_hbm, feat_ref), (bits_hbm, bits_ref), (weight_hbm, weight_ref),
+            )
         )
     ]
     for load in loads:
@@ -146,6 +149,8 @@
     i1 = lax.broadcasted_iota(jnp.int32, (n, n), 1)
     placed = (i1 // 128) * 128 + (i1 % 16) * 8 + (i1 % 128) // 16
     order = (i0 == placed).astype(F32).astype(BF16)
+    for load in loads[:3]:
+        load.wait()
     deg_row = deg_ref[...].astype(F32)
     deg_col = jnp.sum(jnp.where(i0 == i1, deg_row, 0.0), axis=1, keepdims=True)
 
@@ -167,8 +172,8 @@
     plan_copy = pltpu.make_async_copy(plan, plan_smem, plan_s)
     plan_copy.start()
 
-    loads[0].wait()
-    loads[1].wait()
+    loads[3].wait()
+    loads[4].wait()
     grads[c] = (cot_ref[...].astype(F32) / deg_col).astype(BF16)
     feats[r] = dot(feat_ref[...], order, ((0,), (0,))).astype(BF16)
 
@@ -178,28 +183,23 @@
         q = (r + i) % n_row
         return q, copy_to(feats.at[r], feats.at[r], feat_s.at[q], feat_r.at[r], (q, c))
 
-    def grad_copy(k):
-        zz = (2 - z // 2, mate)[k]
-        return copy_to(grads.at[c], grads.at[c], grad_s.at[k], grad_r.at[c], at_z(zz))
-
-    def on_copy(i):
-        q = flip(i) * 2 + core
-        return copy_to(grads.at[q], grads.at[q], on_s.at[i], grad_r.at[q], at_z(mate))
+    def grad_copy(i):
+        return copy_to(grads.at[c], grads.at[c], grad_s.at[i], grad_r.at[c], at_z(flip(i)))
 
     def relay_copy(q):
         return copy_to(grads.at[q], grads.at[q], relay_s.at[q // 2], grad_r.at[q], sibling)
 
     for i in range(1, n_row):
         feat_copy(i)[1].start()
-    for k in range(2):
-        grad_copy(k).start()
+    for i in (3, 2, 1):
+        grad_copy(i).start()
     relay_copy(c).start()
 
     def arrive(ref, sem, slot):
         copy_to(ref.at[slot], ref.at[slot], sem.at[slot], sem.at[slot], sibling).wait_recv()
 
     plan_copy.wait()
-    loads[2].wait()
+    loads[5].wait()
     zero = jnp.zeros((8, 128), jnp.int32)
     for b in range(8):
         prefix[0, b] = zero
@@ -228,14 +228,6 @@
 
     lax.fori_loop(0, trows, place_row, 0)
 
-    @pl.when(inner)
-    def _():
-        for i in (3, 2):
-            q = flip(i) * 2 + core
-            arrive(grads, grad_r, q)
-            on_copy(i).start()
-            relay_copy(q).start()
-
     for i in range(1, n_row):
         arrive(feats, feat_r, (r + i) % n_row)
 
@@ -282,15 +274,10 @@
     sums[mate] = paired(mate).astype(BF16)
     sum_copy(1).start()
 
-    arrive(grads, grad_r, mate * 2 + core)
-    relay_copy(mate * 2 + core).start()
-
-    @pl.when(end)
-    def _():
-        for i in (2, 3):
-            q = flip(i) * 2 + core
-            arrive(grads, grad_r, q)
-            relay_copy(q).start()
+    for i in (1, 2, 3):
+        q = flip(i) * 2 + core
+        arrive(grads, grad_r, q)
+        relay_copy(q).start()
 
     for i in range(n_z):
         arrive(grads, grad_r, flip(i) * 2 + 1 - core)
@@ -347,7 +334,13 @@
     for i in range(1, n_z):
         w2_copy(i).start()
 
-    loads[3].wait()
+    for i in range(1, n_z):
+        arrive(w_mid, w2_r, (z + i) % n_z)
+    w_all[me] = jnp.sum(w_mid[...].astype(F32), axis=0).astype(BF16)
+    for i in range(1, n_plane):
+        w3_copy(i).start()
+
+    loads[6].wait()
     total = back[r].astype(F32)
     for i in range(1, n_row):
         q = (r + i) % n_row
@@ -356,12 +349,6 @@
     ordered = dot(order, total.astype(BF16)).astype(BF16)
     igrad_ref[...] = dot(ordered, weight_ref[...], ((1,), (1,))).astype(BF16)
 
-    for i in range(1, n_z):
-        arrive(w_mid, w2_r, (z + i) % n_z)
-    w_all[me] = jnp.sum(w_mid[...].astype(F32), axis=0).astype(BF16)
-    for i in range(1, n_plane):
-        w3_copy(i).start()
-
     total = paired(z)
     for k in range(2):
         arrive(arrived, sum_r, k)
@@ -376,14 +363,13 @@
     for i in range(1, n_row):
         feat_copy(i)[1].wait_send()
         back_copy((r + i) % n_row).wait_send()
-    for k in range(2):
-        grad_copy(k).wait_send()
+    for i in (1, 2, 3):
+        grad_copy(i).wait_send()
     sum_copy(1).wait_send()
 
     @pl.when(inner)
     def _():
         for i in (2, 3):
-            on_copy(i).wait_send()
             sum_copy(i).wait_send()
 
     @pl.when(end)
@@ -415,29 +401,32 @@
     return pl.pallas_call(
         functools.partial(layer_kernel, n_row, n_z),
         out_shape=(tile, jax.ShapeDtypeStruct((width, width), F32), tile),
-        in_specs=[pl.BlockSpec(memory_space=VMEM)] * 4 + [pl.BlockSpec(memory_space=pl.ANY)] * 4,
+        in_specs=[pl.BlockSpec(memory_space=VMEM)] + [pl.BlockSpec(memory_space=pltpu.HBM)] * 7,
         out_specs=(pl.BlockSpec(memory_space=VMEM),) * 3,
         scratch_shapes=[
             pltpu.VMEM((n * n_row, n * n_col), BF16),
             pltpu.VMEM((slots + 1, 8, 8, 128), jnp.int32),
             pltpu.VMEM((2, slots), jnp.int32),
             pltpu.SMEM((2, slots), jnp.int32),
+            pltpu.VMEM((1, slots), jnp.int32),
+            pltpu.VMEM((1, slots), jnp.int32),
+            pltpu.VMEM((1, n), jnp.int32),
             pltpu.VMEM(bits.shape, jnp.int32),
             pltpu.VMEM((n, width), BF16),
             pltpu.VMEM((n, width), BF16),
             pltpu.VMEM((width, width), BF16),
-            sems(4), pltpu.SemaphoreType.DMA,
+            sems(7), pltpu.SemaphoreType.DMA,
             block(n_row), block(n_col), block(n_col), block(n_z), block(n_z), block(n_z), block(2),
             block(n_row), block(n_row), slab(n_plane), slab(n_plane), slab(n_z), slab(n_plane),
-            sems(n_row), sems(n_row), sems(2), sems(n_col), sems(n_z), sems(4), sems(n_z), sems(n_z),
+            sems(n_row), sems(n_row), sems(n_z), sems(n_col), sems(n_z), sems(n_z), sems(n_z),
             sems(n_z), sems(2), sems(n_z), sems(n_row), sems(n_row),
             sems(n_plane), sems(n_plane), sems(n_z), sems(n_z), sems(n_plane), sems(n_plane),
         ],
         compiler_params=pltpu.CompilerParams(
-            collective_id=0, has_side_effects=True, vmem_limit_bytes=64 * 2**20
+            collective_id=0, has_side_effects=True, vmem_limit_bytes=48 * 2**20
         ),
         name="layer",
-    )(rows, cols, count, degrees, bits, features, cotangent, weight)
+    )(count, rows, cols, degrees, bits, features, cotangent, weight)
 
 
 def swap_order(x, a, b):

time: 46.4 us -> 46.9 us (1.011)
  local copies, waits for them, and re-layouts: 4.8 us -> 8.35 us
  Pallas kernels: 40 us -> 36.9 us
    unnamed x3 -> x17, local copies, waits for them, and re-layouts: 4.8 us -> 8.35 us
    pallas_call x1, Pallas kernels: 40 us -> 36.9 us  [layer(): pl.pallas_call(functools.partial(layer_kernel, n_row, n_z), out_shape=(ti...]
where the time goes in v5:
time: 46.9 us; the launch traced here: 46.6 us
  Pallas kernels  36.9 us (79%)
  local copies, waits for them, and re-layouts  8.35 us (18%)
  between operations  1.3 us (3%)
    pallas_call x1, Pallas kernels, layer(): pl.pallas_call(functools.partial(layer_kernel, n_row, n_z), out_shape=(ti...  36.9 us
    unnamed x17, local copies, waits for them, and re-layouts  8.35 us

profile of v5, /device:TPU:0, one launch (start us, length us, event | category | flops | bytes accessed | tf_op | source)
XLA Modules:
  0.0 46.6 jit_solution(5547112454129508259)
XLA Ops:
  1.3 0.0 copy-start
  1.3 1.6 %copy-done = s32[1,1,256,16,128]{4,3,2,1,0:T(8,128)S(1)} copy-done((s32[1,1,256,16,128]{4,3,2,1,0:T(8,128)S(1)}, s32[1,1,256,16,128]{4,3,2,1,0:T(8,128)}, u32[]{:S(2)}) %copy-start) | copy-done | bytes 2097176
  2.9 0.0 copy-start.1
  2.9 0.9 %copy-done.1 = bf16[256,256]{1,0:T(8,128)(2,1)S(1)} copy-done((bf16[256,256]{1,0:T(8,128)(2,1)S(1)}, bf16[256,256]{1,0:T(8,128)(2,1)}, u32[]{:S(2)}) %copy-start.1) | copy-done | bytes 131096
  3.8 0.0 copy-start.2
  3.8 0.9 %copy-done.2 = bf16[256,256]{1,0:T(8,128)(2,1)S(1)} copy-done((bf16[256,256]{1,0:T(8,128)(2,1)S(1)}, bf16[256,256]{1,0:T(8,128)(2,1)}, u32[]{:S(2)}) %copy-start.2) | copy-done | bytes 131096
  4.7 0.0 copy-start.3
  4.7 0.9 %copy-done.3 = bf16[256,256]{1,0:T(8,128)(2,1)S(1)} copy-done((bf16[256,256]{1,0:T(8,128)(2,1)S(1)}, bf16[256,256]{1,0:T(8,128)(2,1)}, u32[]{:S(2)}) %copy-start.3) | copy-done | bytes 131096
  5.6 0.0 copy-start.4
  5.6 0.7 %copy-done.4 = s32[1,1,256]{2,1,0:T(1,128)S(1)} copy-done((s32[1,1,256]{2,1,0:T(1,128)S(1)}, s32[1,1,256]{2,1,0:T(1,128)}, u32[]{:S(2)}) %copy-start.4) | copy-done | bytes 1048
  6.3 0.0 copy-start.5
  6.3 0.7 %copy-done.5 = s32[1,1,256]{2,1,0:T(1,128)S(1)} copy-done((s32[1,1,256]{2,1,0:T(1,128)S(1)}, s32[1,1,256]{2,1,0:T(1,128)}, u32[]{:S(2)}) %copy-start.5) | copy-done | bytes 1048
  6.9 0.0 copy-start.6
  6.9 0.7 %copy-done.6 = s32[256]{0:T(256)S(1)} copy-done((s32[256]{0:T(256)S(1)}, s32[256]{0:T(256)}, u32[]{:S(2)}) %copy-start.6) | copy-done | bytes 1048
  7.6 36.9 %layer.1 = (bf16[256,256]{1,0:T(8,128)(2,1)S(1)}, f32[256,256]{1,0:T(8,128)S(1)}, bf16[256,256]{1,0:T(8,128)(2,1)S(1)}) custom-call(s32[1,1]{1,0:T(1,128)S(6)} %copy.14.count_ref, s32[1,256]{1,0:T(1,128)S(1)} %bitcast.5, s32[1,256]{1,0:T(1,128)S(1)} %bitcast.6, s32[1,256]{1,0:T(1,128)S(1)} %bitcast.7, s32[256,16,128]{2,1,0:T(8,128)S(1)} %bitcast.4, ...), custom_call_target="tpu_custom_call" | custom-call | tf_op jit(solution)/shard_map/layer/pallas_call | solution.py:401
  44.6 0.7 %copy.15 = bf16[256,256]{1,0:T(8,128)(2,1)} copy(bf16[256,256]{1,0:T(8,128)(2,1)S(1)} %get-tuple-element.6) | data formatting | bytes 262144
  45.2 0.7 %copy.16 = f32[256,256]{1,0:T(8,128)} copy(f32[256,256]{1,0:T(8,128)S(1)} %get-tuple-element.7) | data formatting | bytes 524288
  45.9 0.7 %copy.17 = bf16[256,256]{1,0:T(8,128)(2,1)} copy(bf16[256,256]{1,0:T(8,128)(2,1)S(1)} %get-tuple-element.8) | data formatting | bytes 262144
Async XLA Ops:
  1.3 1.6 %copy-start = (s32[1,1,256,16,128]{4,3,2,1,0:T(8,128)S(1)}, s32[1,1,256,16,128]{4,3,2,1,0:T(8,128)}, u32[]{:S(2)}) copy-start(s32[1,1,256,16,128]{4,3,2,1,0:T(8,128)} %param.14) | copy-start | bytes 6291460
  2.9 0.9 %copy-start.1 = (bf16[256,256]{1,0:T(8,128)(2,1)S(1)}, bf16[256,256]{1,0:T(8,128)(2,1)}, u32[]{:S(2)}) copy-start(bf16[256,256]{1,0:T(8,128)(2,1)} %feat_hbm.1) | copy-start | bytes 393220
  3.8 0.9 %copy-start.2 = (bf16[256,256]{1,0:T(8,128)(2,1)S(1)}, bf16[256,256]{1,0:T(8,128)(2,1)}, u32[]{:S(2)}) copy-start(bf16[256,256]{1,0:T(8,128)(2,1)} %cot_hbm.1) | copy-start | bytes 393220
  4.7 0.9 %copy-start.3 = (bf16[256,256]{1,0:T(8,128)(2,1)S(1)}, bf16[256,256]{1,0:T(8,128)(2,1)}, u32[]{:S(2)}) copy-start(bf16[256,256]{1,0:T(8,128)(2,1)} %weight_hbm.1) | copy-start | bytes 393220
  5.6 0.7 %copy-start.4 = (s32[1,1,256]{2,1,0:T(1,128)S(1)}, s32[1,1,256]{2,1,0:T(1,128)}, u32[]{:S(2)}) copy-start(s32[1,1,256]{2,1,0:T(1,128)} %param.12) | copy-start | bytes 3076
  6.3 0.7 %copy-start.5 = (s32[1,1,256]{2,1,0:T(1,128)S(1)}, s32[1,1,256]{2,1,0:T(1,128)}, u32[]{:S(2)}) copy-start(s32[1,1,256]{2,1,0:T(1,128)} %param.13) | copy-start | bytes 3076
  6.9 0.7 %copy-start.6 = (s32[256]{0:T(256)S(1)}, s32[256]{0:T(256)}, u32[]{:S(2)}) copy-start(s32[256]{0:T(256)} %param.10) | copy-start | bytes 3076

commit v6 on v5

--- a/solution.py
+++ b/solution.py
@@ -95,7 +95,7 @@
     count_ref, rows_hbm, cols_hbm, deg_hbm, bits_hbm, feat_hbm, cot_hbm, weight_hbm,
     out_ref, wgrad_ref, igrad_ref,
     at_ref, prefix, plan, plan_smem, rows_ref, cols_ref, deg_ref, bits_ref, feat_ref, cot_ref, weight_ref, load_s, plan_s,
-    feats, grads, part, pair, sums, passed, arrived, back, back_in, w_part, w_in, w_mid, w_all,
+    feats, grads, part, pair, sums, passed, arrived, back, back_sum, back_in, w_part, w_in, w_mid, w_all,
     feat_s, feat_r, grad_s, grad_r, relay_s, pair_s, pair_r, sum_s, sum_r, pass_r, back_s, back_r,
     w1_s, w1_r, w2_s, w2_r, w3_s, w3_r,
 ):
@@ -149,11 +149,34 @@
     i1 = lax.broadcasted_iota(jnp.int32, (n, n), 1)
     placed = (i1 // 128) * 128 + (i1 % 16) * 8 + (i1 % 128) // 16
     order = (i0 == placed).astype(F32).astype(BF16)
-    for load in loads[:3]:
-        load.wait()
+    loads[2].wait()
     deg_row = deg_ref[...].astype(F32)
     deg_col = jnp.sum(jnp.where(i0 == i1, deg_row, 0.0), axis=1, keepdims=True)
-
+    loads[3].wait()
+    grads[c] = (cot_ref[...].astype(F32) / deg_col).astype(BF16)
+
+    pl.semaphore_wait(barrier, n_plane + n_z - 2)
+
+    def feat_copy(i):
+        q = (r + i) % n_row
+        return q, copy_to(feats.at[r], feats.at[r], feat_s.at[q], feat_r.at[r], (q, c))
+
+    def grad_copy(i):
+        return copy_to(grads.at[c], grads.at[c], grad_s.at[i], grad_r.at[c], at_z(flip(i)))
+
+    def relay_copy(q):
+        return copy_to(grads.at[q], grads.at[q], relay_s.at[q // 2], grad_r.at[q], sibling)
+
+    for i in (3, 2, 1):
+        grad_copy(i).start()
+    relay_copy(c).start()
+    loads[4].wait()
+    feats[r] = dot(feat_ref[...], order, ((0,), (0,))).astype(BF16)
+    for i in range(1, n_row):
+        feat_copy(i)[1].start()
+
+    loads[0].wait()
+    loads[1].wait()
     trows = n * n_col // 128
     tcols = n * n_row // 128
     places = trows * tcols
@@ -172,28 +195,6 @@
     plan_copy = pltpu.make_async_copy(plan, plan_smem, plan_s)
     plan_copy.start()
 
-    loads[3].wait()
-    loads[4].wait()
-    grads[c] = (cot_ref[...].astype(F32) / deg_col).astype(BF16)
-    feats[r] = dot(feat_ref[...], order, ((0,), (0,))).astype(BF16)
-
-    pl.semaphore_wait(barrier, n_plane + n_z - 2)
-
-    def feat_copy(i):
-        q = (r + i) % n_row
-        return q, copy_to(feats.at[r], feats.at[r], feat_s.at[q], feat_r.at[r], (q, c))
-
-    def grad_copy(i):
-        return copy_to(grads.at[c], grads.at[c], grad_s.at[i], grad_r.at[c], at_z(flip(i)))
-
-    def relay_copy(q):
-        return copy_to(grads.at[q], grads.at[q], relay_s.at[q // 2], grad_r.at[q], sibling)
-
-    for i in range(1, n_row):
-        feat_copy(i)[1].start()
-    for i in (3, 2, 1):
-        grad_copy(i).start()
-    relay_copy(c).start()
 
     def arrive(ref, sem, slot):
         copy_to(ref.at[slot], ref.at[slot], sem.at[slot], sem.at[slot], sibling).wait_recv()
@@ -274,25 +275,27 @@
     sums[mate] = paired(mate).astype(BF16)
     sum_copy(1).start()
 
+    def add_back(q):
+        lanes = pl.ds(pl.multiple_of(q * n, n), n)
+        return dot(at_ref[:, lanes], grads[q])
+
+    back_sum[...] = add_back(c)
     for i in (1, 2, 3):
         q = flip(i) * 2 + core
         arrive(grads, grad_r, q)
         relay_copy(q).start()
-
+        back_sum[...] += add_back(q)
     for i in range(n_z):
-        arrive(grads, grad_r, flip(i) * 2 + 1 - core)
+        q = flip(i) * 2 + 1 - core
+        arrive(grads, grad_r, q)
+        back_sum[...] += add_back(q)
 
     def back_copy(q):
         return copy_to(back.at[q], back_in.at[r], back_s.at[q], back_r.at[r], (q, c))
 
-    def backward(q):
-        rows = pl.ds(pl.multiple_of(q * n, n), n)
-        back[q] = dot(at_ref[rows, :], grads[...].reshape(n_col * n, -1)).astype(BF16)
-
-    @pl.loop(1, n_row)
-    def _(i):
+    for i in range(1, n_row):
         q = (r + i) % n_row
-        backward(q)
+        back[q] = back_sum[pl.ds(pl.multiple_of(q * n, n), n), :].astype(BF16)
         back_copy(q).start()
 
     @pl.when(inner)
@@ -326,7 +329,6 @@
 
     for i in range(1, n_plane):
         w1_copy(i).start()
-    backward(r)
     w_in[me] = w_part[me]
     for i in range(1, n_plane):
         arrive(w_in, w1_r, (me + i) % n_plane)
@@ -341,7 +343,7 @@
         w3_copy(i).start()
 
     loads[6].wait()
-    total = back[r].astype(F32)
+    total = back_sum[pl.ds(pl.multiple_of(r * n, n), n), :]
     for i in range(1, n_row):
         q = (r + i) % n_row
         arrive(back_in, back_r, q)
@@ -387,6 +389,27 @@
         w3_copy(i).wait_send()
     for i in range(1, n_z):
         w2_copy(i).wait_send()
+
+
+def place_kernel(*refs):
+    n = len(refs) // 2
+    copies = [pltpu.make_async_copy(refs[k], refs[n + k], refs[-1].at[k]) for k in range(n)]
+    for copy in copies:
+        copy.start()
+    for copy in copies:
+        copy.wait()
+
+
+def place(arrays):
+    return pl.pallas_call(
+        place_kernel,
+        out_shape=tuple(jax.ShapeDtypeStruct(x.shape, x.dtype) for x in arrays),
+        in_specs=[pl.BlockSpec(memory_space=pl.ANY)] * len(arrays),
+        out_specs=(pl.BlockSpec(memory_space=pl.ANY),) * len(arrays),
+        scratch_shapes=[pltpu.SemaphoreType.DMA((len(arrays),))],
+        compiler_params=pltpu.CompilerParams(vmem_limit_bytes=64 * 2**20),
+        name="place",
+    )(*arrays)
 
 
 def layer(rows, cols, count, bits, features, cotangent, degrees, weight, n_row, n_z):
@@ -417,13 +440,13 @@
             pltpu.VMEM((width, width), BF16),
             sems(7), pltpu.SemaphoreType.DMA,
             block(n_row), block(n_col), block(n_col), block(n_z), block(n_z), block(n_z), block(2),
-            block(n_row), block(n_row), slab(n_plane), slab(n_plane), slab(n_z), slab(n_plane),
+            block(n_row), pltpu.VMEM((n * n_row, width), F32), block(n_row), slab(n_plane), slab(n_plane), slab(n_z), slab(n_plane),
             sems(n_row), sems(n_row), sems(n_z), sems(n_col), sems(n_z), sems(n_z), sems(n_z),
             sems(n_z), sems(2), sems(n_z), sems(n_row), sems(n_row),
             sems(n_plane), sems(n_plane), sems(n_z), sems(n_z), sems(n_plane), sems(n_plane),
         ],
         compiler_params=pltpu.CompilerParams(
-            collective_id=0, has_side_effects=True, vmem_limit_bytes=48 * 2**20
+            collective_id=0, has_side_effects=True, vmem_limit_bytes=64 * 2**20
         ),
         name="layer",
     )(count, rows, cols, degrees, bits, features, cotangent, weight)
@@ -440,10 +463,11 @@
     n_row, n_col = lax.axis_size("row"), lax.axis_size("col")
     slots = tile_bits.shape[2]
     if n_row == 4 and n_col == 8 and nodes == width and trows * tcols < slots:
-        return layer(
+        results = layer(
             tile_rows[0], tile_cols[0], tile_count, tile_bits[0, 0],
             features, cotangent, degrees.reshape(1, nodes), weight, n_row, n_col // 2,
         )
+        return place(results)
     at = build_adjacency(
         tile_count[0], tile_rows[0, 0], tile_cols[0, 0], tile_bits[0, 0], trows, tcols
     )

time: 46.9 us -> 56.8 us (1.21)
  Pallas kernels: 36.9 us -> 55.4 us
  local copies, waits for them, and re-layouts: 8.35 us -> 0 us
    pallas_call x0 -> x1, Pallas kernels: none -> 17 us  [place(): pl.pallas_call(place_kernel, out_shape=tuple((jax.ShapeDtypeStruct(x.shap...]
    unnamed x17 -> x0, local copies, waits for them, and re-layouts: 8.35 us -> none
    pallas_call x1, Pallas kernels: 36.9 us -> 38.4 us  [layer(): pl.pallas_call(functools.partial(layer_kernel, n_row, n_z), out_shape=(ti...]
where the time goes in v6:
time: 56.8 us; the launch traced here: 56.7 us
  Pallas kernels  55.4 us (98%)
  between operations  1.29 us (2%)
    pallas_call x1, Pallas kernels, layer(): pl.pallas_call(functools.partial(layer_kernel, n_row, n_z), out_shape=(ti...  38.4 us
    pallas_call x1, Pallas kernels, place(): pl.pallas_call(place_kernel, out_shape=tuple((jax.ShapeDtypeStruct(x.shap...  17 us

profile of v6, /device:TPU:0, one launch (start us, length us, event | category | flops | bytes accessed | tf_op | source)
XLA Modules:
  0.0 56.7 jit_solution(6450504580029287132)
XLA Ops:
  1.3 38.4 %layer.1 = (bf16[256,256]{1,0:T(8,128)(2,1)}, f32[256,256]{1,0:T(8,128)}, bf16[256,256]{1,0:T(8,128)(2,1)}) custom-call(s32[1,1]{1,0:T(1,128)S(6)} %copy.11.count_ref, s32[1,256]{1,0:T(1,128)} %bitcast.5, s32[1,256]{1,0:T(1,128)} %bitcast.6, s32[1,256]{1,0:T(1,128)} %bitcast.7, s32[256,16,128]{2,1,0:T(8,128)} %bitcast.4, bf16[256,256]{1,0:T(8,128)(2,1)} %feat_hbm.1, ...), custom_call_target="tpu_custom_call" | custom-call | tf_op jit(solution)/shard_map/layer/pallas_call | solution.py:424
  39.7 17.0 %place.1 = (bf16[256,256]{1,0:T(8,128)(2,1)}, f32[256,256]{1,0:T(8,128)}, bf16[256,256]{1,0:T(8,128)(2,1)}) custom-call(bf16[256,256]{1,0:T(8,128)(2,1)} %get-tuple-element.6.refs_0_, f32[256,256]{1,0:T(8,128)} %get-tuple-element.7.refs_1_, bf16[256,256]{1,0:T(8,128)(2,1)} %get-tuple-element.8.refs_2_), custom_call_target="tpu_custom_call" | custom-call | tf_op jit(solution)/shard_map/place/pallas_call | solution.py:404

commit v7 on v6

--- a/solution.py
+++ b/solution.py
@@ -155,6 +155,8 @@
     loads[3].wait()
     grads[c] = (cot_ref[...].astype(F32) / deg_col).astype(BF16)
 
+    loads[4].wait()
+    feats[r] = dot(feat_ref[...], order, ((0,), (0,))).astype(BF16)
     pl.semaphore_wait(barrier, n_plane + n_z - 2)
 
     def feat_copy(i):
@@ -167,13 +169,11 @@
     def relay_copy(q):
         return copy_to(grads.at[q], grads.at[q], relay_s.at[q // 2], grad_r.at[q], sibling)
 
+    for i in range(1, n_row):
+        feat_copy(i)[1].start()
     for i in (3, 2, 1):
         grad_copy(i).start()
     relay_copy(c).start()
-    loads[4].wait()
-    feats[r] = dot(feat_ref[...], order, ((0,), (0,))).astype(BF16)
-    for i in range(1, n_row):
-        feat_copy(i)[1].start()
 
     loads[0].wait()
     loads[1].wait()
@@ -268,23 +268,38 @@
 
     @pl.when(end)
     def _():
-        for i in (3, 2):
-            sums[flip(i)] = paired(flip(i)).astype(BF16)
-            pass_copy(i).start()
+        sums[flip(3)] = paired(flip(3)).astype(BF16)
+        pass_copy(3).start()
+        sums[flip(2)] = paired(flip(2)).astype(BF16)
 
     sums[mate] = paired(mate).astype(BF16)
-    sum_copy(1).start()
+
+    @pl.when(inner)
+    def _():
+        sum_copy(1).start()
 
     def add_back(q):
         lanes = pl.ds(pl.multiple_of(q * n, n), n)
         return dot(at_ref[:, lanes], grads[q])
 
     back_sum[...] = add_back(c)
+
+    @pl.when(end)
+    def _():
+        pass_copy(3).wait_send()
+        pass_copy(2).start()
+
     for i in (1, 2, 3):
         q = flip(i) * 2 + core
         arrive(grads, grad_r, q)
         relay_copy(q).start()
         back_sum[...] += add_back(q)
+
+    @pl.when(end)
+    def _():
+        pass_copy(2).wait_send()
+        sum_copy(1).start()
+
     for i in range(n_z):
         q = flip(i) * 2 + 1 - core
         arrive(grads, grad_r, q)
@@ -298,14 +313,16 @@
         back[q] = back_sum[pl.ds(pl.multiple_of(q * n, n), n), :].astype(BF16)
         back_copy(q).start()
 
+    def add_passed(i):
+        zz = flip(i)
+        total = paired(zz)
+        arrive(passed, pass_r, zz)
+        sums[zz] = (total + passed[zz].astype(F32)).astype(BF16)
+        sum_copy(i).start()
+
     @pl.when(inner)
     def _():
-        for i in (2, 3):
-            zz = flip(i)
-            total = paired(zz)
-            arrive(passed, pass_r, zz)
-            sums[zz] = (total + passed[zz].astype(F32)).astype(BF16)
-            sum_copy(i).start()
+        add_passed(2)
 
     local = dot(part[0], grads[0])
     for q in range(1, n_col):
@@ -329,6 +346,11 @@
 
     for i in range(1, n_plane):
         w1_copy(i).start()
+
+    @pl.when(inner)
+    def _():
+        add_passed(3)
+
     w_in[me] = w_part[me]
     for i in range(1, n_plane):
         arrive(w_in, w1_r, (me + i) % n_plane)
@@ -374,11 +396,6 @@
         for i in (2, 3):
             sum_copy(i).wait_send()
 
-    @pl.when(end)
-    def _():
-        for i in (2, 3):
-            pass_copy(i).wait_send()
-
     for i in range(n_z):
         zz = (z + i) % n_z
         relay_copy(zz * 2 + core).wait_send()
@@ -393,20 +410,16 @@
 
 def place_kernel(*refs):
     n = len(refs) // 2
-    copies = [pltpu.make_async_copy(refs[k], refs[n + k], refs[-1].at[k]) for k in range(n)]
-    for copy in copies:
-        copy.start()
-    for copy in copies:
-        copy.wait()
+    for k in range(n):
+        refs[n + k][...] = refs[k][...]
 
 
 def place(arrays):
     return pl.pallas_call(
         place_kernel,
         out_shape=tuple(jax.ShapeDtypeStruct(x.shape, x.dtype) for x in arrays),
-        in_specs=[pl.BlockSpec(memory_space=pl.ANY)] * len(arrays),
-        out_specs=(pl.BlockSpec(memory_space=pl.ANY),) * len(arrays),
-        scratch_shapes=[pltpu.SemaphoreType.DMA((len(arrays),))],
+        in_specs=[pl.BlockSpec(memory_space=VMEM)] * len(arrays),
+        out_specs=(pl.BlockSpec(memory_space=VMEM),) * len(arrays),
         compiler_params=pltpu.CompilerParams(vmem_limit_bytes=64 * 2**20),
         name="place",
     )(*arrays)

time: 56.8 us -> 43.1 us (0.76)
  Pallas kernels: 55.4 us -> 41.6 us
    pallas_call x1, Pallas kernels: 17 us -> 1.85 us  [place(): pl.pallas_call(place_kernel, out_shape=tuple((jax.ShapeDtypeStruct(x.shap...]
    pallas_call x1, Pallas kernels: 38.4 us -> 39.8 us  [layer(): pl.pallas_call(functools.partial(layer_kernel, n_row, n_z), out_shape=(ti...]
where the time goes in v7:
time: 43.1 us; the launch traced here: 42.9 us
  Pallas kernels  41.6 us (97%)
  between operations  1.29 us (3%)
    pallas_call x1, Pallas kernels, layer(): pl.pallas_call(functools.partial(layer_kernel, n_row, n_z), out_shape=(ti...  39.8 us
    pallas_call x1, Pallas kernels, place(): pl.pallas_call(place_kernel, out_shape=tuple((jax.ShapeDtypeStruct(x.shap...  1.85 us

profile of v7, /device:TPU:0, one launch (start us, length us, event | category | flops | bytes accessed | tf_op | source)
XLA Modules:
  0.0 42.9 jit_solution(7519101727221621097)
XLA Ops:
  1.3 39.8 %layer.1 = (bf16[256,256]{1,0:T(8,128)(2,1)}, f32[256,256]{1,0:T(8,128)}, bf16[256,256]{1,0:T(8,128)(2,1)}) custom-call(s32[1,1]{1,0:T(1,128)S(6)} %copy.11.count_ref, s32[1,256]{1,0:T(1,128)} %bitcast.5, s32[1,256]{1,0:T(1,128)} %bitcast.6, s32[1,256]{1,0:T(1,128)} %bitcast.7, s32[256,16,128]{2,1,0:T(8,128)} %bitcast.4, bf16[256,256]{1,0:T(8,128)(2,1)} %feat_hbm.1, ...), custom_call_target="tpu_custom_call" | custom-call | tf_op jit(solution)/shard_map/layer/pallas_call | solution.py:437
  41.1 1.8 %place.1 = (bf16[256,256]{1,0:T(8,128)(2,1)}, f32[256,256]{1,0:T(8,128)}, bf16[256,256]{1,0:T(8,128)(2,1)}) custom-call(bf16[256,256]{1,0:T(8,128)(2,1)} %get-tuple-element.6.refs_0_, f32[256,256]{1,0:T(8,128)} %get-tuple-element.7.refs_1_, bf16[256,256]{1,0:T(8,128)(2,1)} %get-tuple-element.8.refs_2_), custom_call_target="tpu_custom_call" | custom-call | tf_op jit(solution)/shard_map/place/pallas_call | solution.py:418

commit v8 on v7

--- a/solution.py
+++ b/solution.py
@@ -271,34 +271,22 @@
         sums[flip(3)] = paired(flip(3)).astype(BF16)
         pass_copy(3).start()
         sums[flip(2)] = paired(flip(2)).astype(BF16)
+        pass_copy(2).start()
 
     sums[mate] = paired(mate).astype(BF16)
-
-    @pl.when(inner)
-    def _():
-        sum_copy(1).start()
+    sum_copy(1).start()
 
     def add_back(q):
         lanes = pl.ds(pl.multiple_of(q * n, n), n)
         return dot(at_ref[:, lanes], grads[q])
 
     back_sum[...] = add_back(c)
-
-    @pl.when(end)
-    def _():
-        pass_copy(3).wait_send()
-        pass_copy(2).start()
 
     for i in (1, 2, 3):
         q = flip(i) * 2 + core
         arrive(grads, grad_r, q)
         relay_copy(q).start()
         back_sum[...] += add_back(q)
-
-    @pl.when(end)
-    def _():
-        pass_copy(2).wait_send()
-        sum_copy(1).start()
 
     for i in range(n_z):
         q = flip(i) * 2 + 1 - core
@@ -319,10 +307,6 @@
         arrive(passed, pass_r, zz)
         sums[zz] = (total + passed[zz].astype(F32)).astype(BF16)
         sum_copy(i).start()
-
-    @pl.when(inner)
-    def _():
-        add_passed(2)
 
     local = dot(part[0], grads[0])
     for q in range(1, n_col):
@@ -349,7 +333,7 @@
 
     @pl.when(inner)
     def _():
-        add_passed(3)
+        add_passed(2)
 
     w_in[me] = w_part[me]
     for i in range(1, n_plane):
@@ -357,6 +341,10 @@
     w_mid[z] = jnp.sum(w_in[...].astype(F32), axis=0).astype(BF16)
     for i in range(1, n_z):
         w2_copy(i).start()
+
+    @pl.when(inner)
+    def _():
+        add_passed(3)
 
     for i in range(1, n_z):
         arrive(w_mid, w2_r, (z + i) % n_z)
@@ -404,6 +392,12 @@
     for i in range(1, n_plane):
         w1_copy(i).wait_send()
         w3_copy(i).wait_send()
+
+    @pl.when(end)
+    def _():
+        for i in (2, 3):
+            pass_copy(i).wait_send()
+
     for i in range(1, n_z):
         w2_copy(i).wait_send()
 

time: 43.1 us -> 41.7 us (0.968)
  Pallas kernels: 41.6 us -> 40.2 us
    pallas_call x1, Pallas kernels: 39.8 us -> 38.4 us  [layer(): pl.pallas_call(functools.partial(layer_kernel, n_row, n_z), out_shape=(ti...]
where the time goes in v8:
time: 41.7 us; the launch traced here: 41.5 us
  Pallas kernels  40.2 us (96%)
  between operations  1.29 us (3%)
    pallas_call x1, Pallas kernels, layer(): pl.pallas_call(functools.partial(layer_kernel, n_row, n_z), out_shape=(ti...  38.4 us
    pallas_call x1, Pallas kernels, place(): pl.pallas_call(place_kernel, out_shape=tuple((jax.ShapeDtypeStruct(x.shap...  1.85 us

profile of v8, /device:TPU:0, one launch (start us, length us, event | category | flops | bytes accessed | tf_op | source)
XLA Modules:
  0.0 41.5 jit_solution(14058863271803992882)
XLA Ops:
  1.3 38.4 %layer.1 = (bf16[256,256]{1,0:T(8,128)(2,1)}, f32[256,256]{1,0:T(8,128)}, bf16[256,256]{1,0:T(8,128)(2,1)}) custom-call(s32[1,1]{1,0:T(1,128)S(6)} %copy.11.count_ref, s32[1,256]{1,0:T(1,128)} %bitcast.5, s32[1,256]{1,0:T(1,128)} %bitcast.6, s32[1,256]{1,0:T(1,128)} %bitcast.7, s32[256,16,128]{2,1,0:T(8,128)} %bitcast.4, bf16[256,256]{1,0:T(8,128)(2,1)} %feat_hbm.1, ...), custom_call_target="tpu_custom_call" | custom-call | tf_op jit(solution)/shard_map/layer/pallas_call | solution.py:431
  39.7 1.8 %place.1 = (bf16[256,256]{1,0:T(8,128)(2,1)}, f32[256,256]{1,0:T(8,128)}, bf16[256,256]{1,0:T(8,128)(2,1)}) custom-call(bf16[256,256]{1,0:T(8,128)(2,1)} %get-tuple-element.6.refs_0_, f32[256,256]{1,0:T(8,128)} %get-tuple-element.7.refs_1_, bf16[256,256]{1,0:T(8,128)(2,1)} %get-tuple-element.8.refs_2_), custom_call_target="tpu_custom_call" | custom-call | tf_op jit(solution)/shard_map/place/pallas_call | solution.py:412
